TPU v7x, 256 devices: a whole 4x4x8 slice. The times are simulated.
256 devices in a mesh: tgt: 32 (over z, x), src: 8 (over y, core).
Axes of the slice: x: 4, y: 4, z: 8, core: 2. Of those that a mesh axis runs over, the one named last changes fastest.
Arguments:
- sources: bfloat16 [1024, 1024], P('src', 'tgt'), as said below
- targets: bfloat16 [32768, 1024], P('tgt'), as said below
- fwd_idx: int32 [1024, 16], P('src'), may hold values from 0 to 32767
- bwd_idx: int32 [32768, 16], P('tgt'), may hold values from 0 to 1023
- bwd_len: int32 [32768], P('tgt'), may hold values from 1 to 16
Outputs:
- margin: float32 [1024, 16], P('src')
Inputs may be any that keep to these rules, and one draw needn't show every extreme that they name: `sources`: entries are non-negative. `targets`: entries are non-negative.
All inputs are finite; a program needn't handle non-finite values.
Results may differ from a plain program's by a relative error of at most 0.0003.
Values may be sent and summed in bfloat16 or wider, within the bound.
No kernel may reach another device: no remote copies, remote signals or barrier semaphores. Data moves between devices by JAX's collectives and lax.ppermute only.
A program may use at most 64 MiB of HBM per device.

v0:
```python
import jax
import jax.numpy as jnp
from jax import lax
from jax.sharding import PartitionSpec as P


def ratio_margin(cand_cos, cand_bwd):
    fwd_mean = jnp.mean(cand_cos, axis=1)
    return cand_cos / ((fwd_mean[:, None] + cand_bwd) * 0.5)


def body(sources, targets, fwd_idx, bwd_idx, bwd_len):
    tgt_rows = targets.shape[0]
    group_rows = fwd_idx.shape[0]
    neighbours = fwd_idx.shape[1]
    tgt_float = targets.astype(jnp.float32)
    tgt_scale = lax.rsqrt(jnp.sum(tgt_float * tgt_float, axis=1) + 1e-06)
    contract = (((1,), (1,)), ((), ()))
    gathered = lax.all_gather(sources, "tgt", axis=1, tiled=True)
    src_float = gathered.astype(jnp.float32)
    src_scale = lax.rsqrt(jnp.sum(src_float * src_float, axis=1) + 1e-06)
    products = lax.dot_general(targets, gathered, contract, preferred_element_type=jnp.float32)
    scores = products * tgt_scale[:, None] * src_scale[None, :]
    group_index = lax.axis_index("src")
    local_src = bwd_idx - group_index * group_rows
    counted = jnp.arange(neighbours)[None, :] < bwd_len[:, None]
    src_column = jnp.arange(group_rows, dtype=jnp.int32)
    slot_src = jnp.where(counted, local_src, -1).T

    def add_backward(total, slot_column):
        match = slot_column[:, None] == src_column[None, :]
        return (total + jnp.sum(jnp.where(match, scores, 0.0), axis=1), None)

    back_term, unused = lax.scan(add_backward, jnp.zeros((tgt_rows,), jnp.float32), slot_src)
    back_total = lax.psum(back_term, "src")
    bwd_mean = back_total / bwd_len.astype(jnp.float32)
    shard_index = lax.axis_index("tgt")
    local_tgt = (fwd_idx - shard_index * tgt_rows).T
    tgt_column = jnp.arange(tgt_rows, dtype=jnp.int32)

    def pick_forward(slot_column):
        match = tgt_column[:, None] == slot_column[None, :]
        cos_part = jnp.sum(jnp.where(match, scores, 0.0), axis=0)
        bwd_part = jnp.sum(jnp.where(match, bwd_mean[:, None], 0.0), axis=0)
        return (cos_part, bwd_part)

    cos_slots, bwd_slots = lax.map(pick_forward, local_tgt)
    cos_term = cos_slots.T
    bwd_term = bwd_slots.T
    cand_cos, cand_bwd = lax.psum((cos_term, bwd_term), "tgt")
    return ratio_margin(cand_cos, cand_bwd)


def solution(mesh):
    in_specs = (P("src", "tgt"), P("tgt", None), P("src", None), P("tgt", None), P("tgt"))
    out_specs = P("src", None)
    return jax.shard_map(body, mesh=mesh, in_specs=in_specs, out_specs=out_specs, check_vma=False)
```

profile of v0, /device:TPU:2, one launch (start us, length us, event | category | flops | bytes accessed | tf_op | source)
XLA Modules:
  0.0 215.7 jit_solution(9530062625518758813)
XLA Ops:
  0.0 51.9 %all_gather.3 = bf16[128,1024]{0,1:T(8,128)(2,1)S(1)} all-gather(bf16[128,32]{0,1:T(8,128)(2,1)} %param.9), channel_id=1, replica_groups=mesh['tgt'=32,'src'=8] {'tgt'}, dimensions={1}, use_global_device_ids=true | all-gather | bytes 270336 | tf_op jit(solution)/shard_map/all_gather | solution.py:19
  52.0 2.1 multiply_reduce_fusion
  54.2 0.7 fusion.8
  54.9 6.7 %while.25 = (s32[]{:T(128)}, f32[1024]{0:T(1024)S(1)}, s32[16,1024]{1,0:T(8,128)S(1)}, f32[1024,128]{1,0:T(8,128)S(1)}, s32[]{:T(128)}, /*index=5*/s32[]{:T(128)}) while((s32[]{:T(128)}, f32[1024]{0:T(1024)S(1)}, s32[16,1024]{1,0:T(8,128)S(1)}, f32[1024,128]{1,0:T(8,128)S(1)}, s32[]{:T(128)}, /*index=5*/s32[]{:T(128)}) %tuple.41), condition=%wide.region_4.5_spmd.clone, body=%wide.region_2.4_spmd.clone.sunk | while | flops 394243 | bytes 553043 | solution.py:34
  55.0 0.4 select_reduce_fusion.2
  55.4 0.4 select_reduce_fusion.2
  55.8 0.4 select_reduce_fusion.2
  56.2 0.4 select_reduce_fusion.2
  56.6 0.4 select_reduce_fusion.2
  57.1 0.4 select_reduce_fusion.2
  57.5 0.4 select_reduce_fusion.2
  57.9 0.4 select_reduce_fusion.2
  58.3 0.4 select_reduce_fusion.2
  58.7 0.4 select_reduce_fusion.2
  59.1 0.4 select_reduce_fusion.2
  59.6 0.4 select_reduce_fusion.2
  60.0 0.4 select_reduce_fusion.2
  60.4 0.4 select_reduce_fusion.2
  60.8 0.4 select_reduce_fusion.2
  61.2 0.4 select_reduce_fusion.2
  61.6 12.4 %psum.21 = f32[1024]{0:T(1024)S(1)} all-reduce(f32[1024]{0:T(1024)S(1)} %get-tuple-element.70), channel_id=1, replica_groups=mesh['tgt'=32,'src'=8] {'src'}, use_global_device_ids=true, to_apply=%region_5.6 | all-reduce | flops 1024 | bytes 8192 | tf_op jit(solution)/shard_map/psum | solution.py:35
  74.1 5.2 %while.24 = (s32[]{:T(128)}, f32[16,128]{1,0:T(8,128)S(1)}, f32[16,128]{1,0:T(8,128)S(1)}, s32[16,128]{1,0:T(8,128)S(1)}, f32[1024,128]{1,0:T(8,128)S(1)}, /*index=5*/f32[1024]{0:T(1024)S(1)}, s32[]{:T(128)}, s32[]{:T(128)}) while((s32[]{:T(128)}, f32[16,128]{1,0:T(8,128)S(1)}, f32[16,128]{1,0:T(8,128)S(1)}, ...), condition=%wide.region_9.10_spmd.clone, body=%wide.region_6.9_spmd.clone.sunk | while | flops 655106 | bytes 533089 | solution.py:47
  74.1 0.2 fusion.12
  74.5 0.2 fusion.12
  74.8 0.2 fusion.12
  75.1 0.2 fusion.12
  75.4 0.2 fusion.12
  75.8 0.2 fusion.12
  76.1 0.2 fusion.12
  78.4 0.2 fusion.12
  79.3 135.7 %all-reduce = (f32[128,16]{0,1:T(8,128)S(1)}, f32[128,16]{0,1:T(8,128)S(1)}) all-reduce(f32[128,16]{0,1:T(8,128)S(1)} %bitcast.24, f32[128,16]{0,1:T(8,128)S(1)} %bitcast.25), channel_id=1, replica_groups=mesh['tgt'=32,'src'=8] {'tgt'}, use_global_device_ids=true, to_apply=%region_10.11 | all-reduce | flops 4096 | bytes 32768 | tf_op jit(solution)/shard_map/psum | solution.py:50
  215.1 0.6 multiply_divide_fusion
  (107 shorter events, 3.6 us)
Async XLA Ops:
  0.0 54.1 %copy-start = (bf16[1024,1024]{1,0:T(8,128)(2,1)S(1)}, bf16[1024,1024]{1,0:T(8,128)(2,1)}, u32[]{:S(2)}) copy-start(bf16[1024,1024]{1,0:T(8,128)(2,1)} %param.10) | copy-start | bytes 6291460
  52.0 2.9 %copy-start.1 = (s32[1024,16]{0,1:T(8,128)S(1)}, s32[1024,16]{0,1:T(8,128)}, u32[]{:S(2)}) copy-start(s32[1024,16]{0,1:T(8,128)} %param.12) | copy-start | bytes 196612
  52.0 2.9 %copy-start.2 = (s32[1024]{0:T(1024)S(1)}, s32[1024]{0:T(1024)}, u32[]{:S(2)}) copy-start(s32[1024]{0:T(1024)} %param.13) | copy-start | bytes 12292
  54.9 19.2 %copy-start.3 = (s32[128,16]{0,1:T(8,128)S(1)}, s32[128,16]{0,1:T(8,128)}, u32[]{:S(2)}) copy-start(s32[128,16]{0,1:T(8,128)} %param.11) | copy-start | bytes 24580
where the time goes:
time: 219 us; the launch traced here: 216 us
  blocking collectives  200 us (91%)
  other arithmetic  12.5 us (6%)
    psum x1, blocking collectives, body(): cand_cos, cand_bwd = lax.psum((cos_term, bwd_term), 'tgt')  136 us
    all_gather x1, blocking collectives, body(): gathered = lax.all_gather(sources, 'tgt', axis=1, tiled=True)  51.9 us
    psum x1, blocking collectives, body(): back_total = lax.psum(back_term, 'src')  12.4 us
    reduce_sum x16, other arithmetic, add_backward(): return (total + jnp.sum(jnp.where(match, scores, 0.0), axis=1), None)  5.79 us

commit v1 on v0

v1 whole, which is shorter than its diff:
```python
import jax
import jax.numpy as jnp
from jax import lax
from jax.sharding import Mesh, PartitionSpec as P

Z, X, Y, CORE = 8, 4, 4, 2
TGT = ("z", "x")
SRC = ("y", "core")


def spread(block, axes, count):
    copies = jnp.broadcast_to(block[None], (count,) + block.shape)
    return lax.all_to_all(copies, axes, 0, 0)


def body(sources, targets, fwd_idx, bwd_idx, bwd_len):
    tgt_rows, features = targets.shape
    group_rows, neighbours = fwd_idx.shape
    tgt_float = targets.astype(jnp.float32)
    tgt_scale = lax.rsqrt(jnp.sum(tgt_float * tgt_float, axis=1) + 1e-06)
    gathered = spread(sources.T, TGT, Z * X).reshape(features, group_rows)
    src_float = gathered.astype(jnp.float32)
    src_scale = lax.rsqrt(jnp.sum(src_float * src_float, axis=0) + 1e-06)
    products = jnp.dot(targets, gathered, preferred_element_type=jnp.float32)
    scores = products * tgt_scale[:, None] * src_scale[None, :]
    local_src = bwd_idx - lax.axis_index(SRC) * group_rows
    counted = jnp.arange(neighbours)[None, :] < bwd_len[:, None]
    src_column = jnp.arange(group_rows, dtype=jnp.int32)
    slot_src = jnp.where(counted, local_src, -1).T

    def add_backward(total, slot_column):
        match = slot_column[:, None] == src_column[None, :]
        return (total + jnp.sum(jnp.where(match, scores, 0.0), axis=1), None)

    back_term, unused = lax.scan(add_backward, jnp.zeros((tgt_rows,), jnp.float32), slot_src)
    back_total = jnp.sum(spread(back_term, SRC, Y * CORE), axis=0)
    bwd_mean = back_total / bwd_len.astype(jnp.float32)
    local_tgt = (fwd_idx - lax.axis_index(TGT) * tgt_rows).T
    tgt_column = jnp.arange(tgt_rows, dtype=jnp.int32)

    def pick_forward(slot_column):
        match = tgt_column[:, None] == slot_column[None, :]
        cos_part = jnp.sum(jnp.where(match, scores, 0.0), axis=0)
        bwd_part = jnp.sum(jnp.where(match, bwd_mean[:, None], 0.0), axis=0)
        return (cos_part, bwd_part)

    cos_slots, bwd_slots = lax.map(pick_forward, local_tgt)
    picked = jnp.stack([cos_slots, bwd_slots])
    picked = jnp.sum(spread(picked, "x", X), axis=0)
    picked = jnp.sum(spread(picked, "z", Z), axis=0)
    cand_cos, cand_bwd = picked[0], picked[1]
    fwd_mean = jnp.mean(cand_cos, axis=0)
    return (cand_cos / ((fwd_mean[None, :] + cand_bwd) * 0.5)).T


def solution(mesh):
    grid = Mesh(mesh.devices.reshape(Z, X, Y, CORE), TGT + SRC)
    in_specs = (P(SRC, TGT), P(TGT, None), P(SRC, None), P(TGT, None), P(TGT))
    return jax.shard_map(body, mesh=grid, in_specs=in_specs, out_specs=P(SRC, None), check_vma=False)
```

time: 219 us -> 69.1 us (0.32); the launches traced: 216 us -> 68.8 us
  blocking collectives: 200 us -> 20.2 us
  starting transfers between devices: 0 us -> 16.1 us
  waiting for transfers between devices: 0 us -> 14.5 us
  local copies, waits for them, and re-layouts: 1.41 us -> 3.62 us
    psum x2 -> x0, blocking collectives: 148 us -> none  [the longest x1 136 us: body(): cand_cos, cand_bwd = lax.psum((cos_term, bwd_term), 'tgt')]
    all_gather x1 -> x0, blocking collectives: 51.9 us -> none  [body(): gathered = lax.all_gather(sources, 'tgt', axis=1, tiled=True)]
    all_to_all x0 -> x2, blocking collectives: none -> 20.2 us  [spread(): return lax.all_to_all(copies, axes, 0, 0)]
    all_to_all x0 -> x2, starting transfers between devices: none -> 16.1 us  [spread(): return lax.all_to_all(copies, axes, 0, 0)]
    all_to_all x0 -> x2, waiting for transfers between devices: none -> 14.5 us  [spread(): return lax.all_to_all(copies, axes, 0, 0)]
    broadcast_in_dim x0 -> x4, local copies, waits for them, and re-layouts: none -> 2.21 us  [spread(): copies = jnp.broadcast_to(block[None], (count,) + block.shape)]
  transfers between devices with their start and end apart: 0 -> 2, of which waited for: 0 -> 2; matrix products, arithmetic and copies ran while one was open for 0% -> 3% of each run, Pallas kernels for 0% -> 0%
where the time goes in v1:
time: 69.1 us; the launch traced here: 68.8 us
  blocking collectives  20.2 us (29%)
  starting transfers between devices  16.1 us (23%)
  waiting for transfers between devices  14.5 us (21%)
  other arithmetic  12.5 us (18%)
  local copies, waits for them, and re-layouts  3.62 us (5%)
  loops' own time  0.97 us (1%)
  matrix products  0.71 us (1%)
    all_to_all x2, blocking collectives, spread(): return lax.all_to_all(copies, axes, 0, 0)  20.2 us
    all_to_all x2, starting transfers between devices, spread(): return lax.all_to_all(copies, axes, 0, 0)  16.1 us
    all_to_all x2, waiting for transfers between devices, spread(): return lax.all_to_all(copies, axes, 0, 0)  14.5 us
    reduce_sum x16, other arithmetic, add_backward(): return (total + jnp.sum(jnp.where(match, scores, 0.0), axis=1), None)  5.79 us
    reduce_sum x16, other arithmetic, pick_forward(): bwd_part = jnp.sum(jnp.where(match, bwd_mean[:, None], 0.0), axis=0)  3.65 us
    broadcast_in_dim x4, local copies, waits for them, and re-layouts, spread(): copies = jnp.broadcast_to(block[None], (count,) + block.shape)  2.21 us
    reduce_sum x1, other arithmetic, body(): tgt_scale = lax.rsqrt(jnp.sum(tgt_float * tgt_float, axis=1) + 1e-06)  2.07 us
  transfers between devices with their start and end apart: 2, of which 2 were waited for; matrix products, arithmetic and copies ran while one was open for 3% of the time, Pallas kernels for 0%

profile of v1, /device:TPU:2, one launch (start us, length us, event | category | flops | bytes accessed | tf_op | source)
XLA Modules:
  0.0 68.8 jit_solution(5798651218332694082)
XLA Ops:
  0.0 1.6 %broadcast_in_dim.43 = bf16[32,32,128]{2,1,0:T(8,128)(2,1)} broadcast(bf16[32,128]{1,0:T(8,128)(2,1)} %bitcast.41), dimensions={1,2} | broadcast | bytes 270336 | tf_op jit(solution)/shard_map/broadcast_in_dim | solution.py:12
  1.6 11.6 %all-to-all-start = ((bf16[32,32,128]{2,1,0:T(8,128)(2,1)}), bf16[32,32,128]{2,1,0:T(8,128)(2,1)S(1)}, u32[]{:S(2)}, u32[]{:S(2)}) async-start(bf16[32,32,128]{2,1,0:T(8,128)(2,1)} %broadcast_in_dim.43), calls=%async_computation | async-start | bytes 524288 | tf_op jit(solution)/shard_map/all_to_all | solution.py:13
  13.2 2.1 %multiply_reduce_fusion = f32[1024]{0:T(1024)S(1)} fusion(bf16[1024,1024]{1,0:T(8,128)(2,1)} %param.10), kind=kLoop, calls=%fused_computation.12 | loop fusion | flops 3144704 | bytes 2101248 | tf_op jit(solution)/shard_map/reduce_sum | solution.py:20
  15.4 9.1 %all-to-all-done = bf16[32,32,128]{2,1,0:T(8,128)(2,1)S(1)} async-done(((bf16[32,32,128]{2,1,0:T(8,128)(2,1)}), bf16[32,32,128]{2,1,0:T(8,128)(2,1)S(1)}, u32[]{:S(2)}, u32[]{:S(2)}) %all-to-all-start) | async-done | bytes 262176 | tf_op jit(solution)/shard_map/all_to_all | solution.py:13
  24.6 0.7 %fusion.8 = f32[1024,128]{1,0:T(8,128)S(1)} fusion(bf16[1024,1024]{1,0:T(8,128)(2,1)S(1)} %copy-done, bf16[1024,128]{1,0:T(8,128)(2,1)S(1)} %bitcast.37, f32[128]{0:T(128)S(1)} %add_rsqrt_fusion.1, f32[1024]{0:T(1024)S(1)} %add_rsqrt_fusion), kind=kOutput, calls=%fused_computation.14 | convolution fusion | flops 268697600 | bytes 2888192 | tf_op jit(solution)/shard_map/dot_general | solution.py:24
  25.3 6.7 %while.25 = (s32[]{:T(128)}, f32[1024]{0:T(1024)S(1)}, s32[16,1024]{1,0:T(8,128)S(1)}, f32[1024,128]{1,0:T(8,128)S(1)}, s32[]{:T(128)}, /*index=5*/s32[]{:T(128)}) while((s32[]{:T(128)}, f32[1024]{0:T(1024)S(1)}, s32[16,1024]{1,0:T(8,128)S(1)}, f32[1024,128]{1,0:T(8,128)S(1)}, s32[]{:T(128)}, /*index=5*/s32[]{:T(128)}) %tuple.41), condition=%wide.region_4.5_spmd.clone, body=%wide.region_2.4_spmd.clone.sunk | while | flops 394243 | bytes 553051 | solution.py:35
  25.3 0.4 select_reduce_fusion.2
  25.8 0.4 select_reduce_fusion.2
  26.2 0.4 select_reduce_fusion.2
  26.6 0.4 select_reduce_fusion.2
  27.0 0.4 select_reduce_fusion.2
  27.4 0.4 select_reduce_fusion.2
  27.8 0.4 select_reduce_fusion.2
  28.3 0.4 select_reduce_fusion.2
  28.7 0.4 select_reduce_fusion.2
  29.1 0.4 select_reduce_fusion.2
  29.5 0.4 select_reduce_fusion.2
  29.9 0.4 select_reduce_fusion.2
  30.4 0.4 select_reduce_fusion.2
  30.8 0.4 select_reduce_fusion.2
  31.2 0.4 select_reduce_fusion.2
  31.6 0.4 select_reduce_fusion.2
  32.0 0.6 broadcast_in_dim.68
  32.6 4.5 %all-to-all-start.1 = ((f32[8,1,1024]{2,1,0:T(1,128)}), f32[8,1,1024]{2,1,0:T(1,128)S(1)}, u32[]{:S(2)}, u32[]{:S(2)}) async-start(f32[8,1,1024]{2,1,0:T(1,128)} %broadcast_in_dim.68), calls=%async_computation.1 | async-start | bytes 65536 | tf_op jit(solution)/shard_map/all_to_all | solution.py:13
  37.1 5.4 %all-to-all-done.1 = f32[8,1,1024]{2,1,0:T(1,128)S(1)} async-done(((f32[8,1,1024]{2,1,0:T(1,128)}), f32[8,1,1024]{2,1,0:T(1,128)S(1)}, u32[]{:S(2)}, u32[]{:S(2)}) %all-to-all-start.1) | async-done | bytes 32800 | tf_op jit(solution)/shard_map/all_to_all | solution.py:13
  42.6 5.2 %while.24 = (s32[]{:T(128)}, f32[16,128]{1,0:T(8,128)S(1)}, f32[16,128]{1,0:T(8,128)S(1)}, s32[16,128]{1,0:T(8,128)S(1)}, f32[1024,128]{1,0:T(8,128)S(1)}, /*index=5*/f32[1024]{0:T(1024)S(1)}, s32[]{:T(128)}, s32[]{:T(128)}) while((s32[]{:T(128)}, f32[16,128]{1,0:T(8,128)S(1)}, f32[16,128]{1,0:T(8,128)S(1)}, ...), condition=%wide.region_9.10_spmd.clone, body=%wide.region_6.9_spmd.clone.sunk | while | flops 655106 | bytes 533097 | solution.py:47
  42.6 0.2 fusion.16
  42.9 0.2 fusion.16
  45.2 0.2 fusion.16
  47.8 8.8 %all_to_all.21 = f32[4,2,16,128]{3,2,1,0:T(8,128)S(1)} all-to-all(f32[4,2,16,128]{3,2,1,0:T(8,128)S(1)} %broadcast_in_dim.69), channel_id=1, replica_groups=mesh['z'=8,'x'=4,'y'=4,'core'=2] {'x'}, dimensions={0} | all-to-all | bytes 131072 | tf_op jit(solution)/shard_map/all_to_all | solution.py:13
  56.6 11.5 %all_to_all.22 = f32[8,2,16,128]{3,2,1,0:T(8,128)S(1)} all-to-all(f32[8,2,16,128]{3,2,1,0:T(8,128)S(1)} %broadcast_in_dim.70), channel_id=1, replica_groups=mesh['z'=8,'x'=4,'y'=4,'core'=2] {'z'}, dimensions={0} | all-to-all | bytes 262144 | tf_op jit(solution)/shard_map/all_to_all | solution.py:13
  68.1 0.6 fusion.12
  (118 shorter events, 4.8 us)
Async XLA Ops:
  0.0 24.6 %copy-start = (bf16[1024,1024]{1,0:T(8,128)(2,1)S(1)}, bf16[1024,1024]{1,0:T(8,128)(2,1)}, u32[]{:S(2)}) copy-start(bf16[1024,1024]{1,0:T(8,128)(2,1)} %param.10) | copy-start | bytes 6291460
  0.0 15.3 %copy-start.1 = (s32[1024,16]{0,1:T(8,128)S(1)}, s32[1024,16]{0,1:T(8,128)}, u32[]{:S(2)}) copy-start(s32[1024,16]{0,1:T(8,128)} %param.12) | copy-start | bytes 196612
  0.0 15.3 %copy-start.2 = (s32[1024]{0:T(1024)S(1)}, s32[1024]{0:T(1024)}, u32[]{:S(2)}) copy-start(s32[1024]{0:T(1024)} %param.13) | copy-start | bytes 12292
  1.6 22.8 %all-to-all-start = ((bf16[32,32,128]{2,1,0:T(8,128)(2,1)}), bf16[32,32,128]{2,1,0:T(8,128)(2,1)S(1)}, u32[]{:S(2)}, u32[]{:S(2)}) async-start(bf16[32,32,128]{2,1,0:T(8,128)(2,1)} %broadcast_in_dim.43), calls=%async_computation | async-start | bytes 524288 | tf_op jit(solution)/shard_map/all_to_all | solution.py:13
  25.3 11.8 %copy-start.3 = (s32[128,16]{0,1:T(8,128)S(1)}, s32[128,16]{0,1:T(8,128)}, u32[]{:S(2)}) copy-start(s32[128,16]{0,1:T(8,128)} %param.11) | copy-start | bytes 24580
  32.6 9.9 %all-to-all-start.1 = ((f32[8,1,1024]{2,1,0:T(1,128)}), f32[8,1,1024]{2,1,0:T(1,128)S(1)}, u32[]{:S(2)}, u32[]{:S(2)}) async-start(f32[8,1,1024]{2,1,0:T(1,128)} %broadcast_in_dim.68), calls=%async_computation.1 | async-start | bytes 65536 | tf_op jit(solution)/shard_map/all_to_all | solution.py:13

commit v2 on v1

v2 whole, which is shorter than its diff:
```python
import jax
import jax.numpy as jnp
from jax import lax
from jax.experimental import pallas as pl
from jax.experimental.pallas import tpu as pltpu
from jax.sharding import Mesh, PartitionSpec as P

Z, X, Y, CORE = 8, 4, 4, 2
TGT = ("z", "x")
SRC = ("y", "core")
LANES = 128
VMEM_BYTES = 24 * 1024 * 1024


def take_rows(rows, index):
    return jnp.take_along_axis(rows, index, axis=0)


def take_lanes(rows, index):
    return jnp.take_along_axis(rows, index, axis=1)


def pick_from_tiles(block, index, first_row, picked):
    tile, row = index >> 3, index & 7
    for i in range(block.shape[0] // 8):
        match = tile == (first_row // 8 + i)
        rows = block[8 * i : 8 * i + 8, :]
        picked = [
            jnp.where(match[8 * h : 8 * h + 8], take_rows(rows, row[8 * h : 8 * h + 8]), picked[h])
            for h in range(len(picked))
        ]
    return picked


def pick_from_table(table, index):
    high, low = index >> 7, index & 127
    picked = [jnp.zeros((8, LANES), jnp.float32)] * 2
    for i in range(table.shape[0]):
        row = jnp.broadcast_to(table[i : i + 1, :], (8, LANES))
        picked = [
            jnp.where(high[8 * h : 8 * h + 8] == i, take_lanes(row, low[8 * h : 8 * h + 8]), picked[h])
            for h in range(2)
        ]
    return jnp.concatenate(picked, axis=0)


def score_kernel(place_ref, src_ref, tgt_ref, scale_ref, bwd_ref, len_ref, fwd_ref, out_ref):
    fwd_local = fwd_ref[...] - place_ref[0]
    src = src_ref[...]
    src_float = src.astype(jnp.float32)
    src_scale = lax.rsqrt(jnp.sum(src_float * src_float, axis=0, keepdims=True) + 1e-06)
    tgt_scale = scale_ref[...]
    slot = lax.broadcasted_iota(jnp.int32, (16, LANES), 0)
    cos = [jnp.zeros((8, LANES), jnp.float32)] * 2
    back = []
    for c in range(tgt_ref.shape[0] // LANES):
        lanes = slice(LANES * c, LANES * c + LANES)
        block = jnp.dot(tgt_ref[lanes, :], src, preferred_element_type=jnp.float32) * src_scale
        cos = pick_from_tiles(block, fwd_local, LANES * c, cos)
        bwd_local = bwd_ref[:, lanes] - place_ref[1]
        zero = [jnp.zeros((8, LANES), jnp.float32)] * 2
        sims = jnp.concatenate(pick_from_tiles(block.T, bwd_local, 0, zero), axis=0)
        length = len_ref[c : c + 1, :]
        total = jnp.sum(jnp.where(slot < length, sims, 0.0), axis=0, keepdims=True)
        back.append(total * tgt_scale[c : c + 1, :] / length.astype(jnp.float32))
    cos = jnp.concatenate(cos, axis=0) * pick_from_table(tgt_scale, fwd_local)
    sent = jnp.concatenate(back + [cos], axis=0)
    for d in range(out_ref.shape[0]):
        out_ref[d] = sent


def mean_kernel(place_ref, got_ref, fwd_ref, out_ref):
    groups = got_ref.shape[0] // X
    table, cos = [], jnp.zeros((16, LANES), jnp.float32)
    for x in range(X):
        total = got_ref[x * groups, :8, :]
        for g in range(1, groups):
            total = total + got_ref[x * groups + g, :8, :]
        table.append(total)
        cos = cos + got_ref[x * groups + place_ref[1], 8:, :]
    bwd = pick_from_table(jnp.concatenate(table, axis=0), fwd_ref[...] - place_ref[0])
    for d in range(out_ref.shape[0]):
        out_ref[d, :16, :] = cos
        out_ref[d, 16:, :] = bwd


def margin_kernel(got_ref, out_ref):
    total = jnp.sum(got_ref[...], axis=0)
    cos, bwd = total[:16], total[16:]
    fwd_mean = jnp.mean(cos, axis=0, keepdims=True)
    out_ref[...] = cos / ((fwd_mean + bwd) * 0.5)


def call(kernel, shape, specs, *args):
    return pl.pallas_call(
        kernel,
        out_shape=jax.ShapeDtypeStruct(shape, jnp.float32),
        in_specs=[pl.BlockSpec(memory_space=s) for s in specs],
        out_specs=pl.BlockSpec(memory_space=pltpu.VMEM),
        compiler_params=pltpu.CompilerParams(vmem_limit_bytes=VMEM_BYTES),
    )(*args)


def body(sources, targets, fwd_idx, bwd_idx, bwd_len):
    tgt_rows, features = targets.shape
    group_rows, neighbours = fwd_idx.shape
    smem, vmem = pltpu.SMEM, pltpu.VMEM
    tgt_index = lax.axis_index(TGT)
    src_index = lax.axis_index(SRC)
    fwd = fwd_idx.T
    copies = jnp.broadcast_to(sources.T[None], (Z * X,) + sources.T.shape)
    gathered = lax.all_to_all(copies, TGT, 0, 0).reshape(features, group_rows)
    tgt_float = targets.astype(jnp.float32)
    tgt_scale = lax.rsqrt(jnp.sum(tgt_float * tgt_float, axis=1) + 1e-06)
    place = jnp.stack([tgt_index * tgt_rows, src_index * group_rows]).astype(jnp.int32)
    sent = call(
        score_kernel, (X * Y * CORE, 24, LANES), [smem] + [vmem] * 6,
        place, gathered, targets, tgt_scale.reshape(-1, LANES), bwd_idx.T, bwd_len.reshape(-1, LANES), fwd,
    )
    got = lax.all_to_all(sent, ("x",) + SRC, 0, 0)
    place = jnp.stack([lax.axis_index("z") * (X * tgt_rows), src_index]).astype(jnp.int32)
    sent = call(mean_kernel, (Z, 32, LANES), [smem] + [vmem] * 2, place, got, fwd)
    got = lax.all_to_all(sent, "z", 0, 0)
    return call(margin_kernel, (neighbours, group_rows), [vmem], got).T


def solution(mesh):
    grid = Mesh(mesh.devices.reshape(Z, X, Y, CORE), TGT + SRC)
    in_specs = (P(SRC, TGT), P(TGT, None), P(SRC, None), P(TGT, None), P(TGT))
    return jax.shard_map(body, mesh=grid, in_specs=in_specs, out_specs=P(SRC, None), check_vma=False)
```

time: 69.1 us -> 59.1 us (0.86)
  the two profiles are of different devices: /device:TPU:2 before, /device:TPU:1 now
where the time goes in v2:
time: 59.1 us; the launch traced here: 58.7 us
  starting transfers between devices  20.2 us (34%)
  waiting for transfers between devices  19.2 us (32%)
  blocking collectives  12 us (20%)
  Pallas kernels  3.4 us (6%)
  other arithmetic  2.22 us (4%)
  local copies, waits for them, and re-layouts  1.59 us (3%)
    all_to_all x1, blocking collectives, body(): got = lax.all_to_all(sent, 'z', 0, 0)  12 us
    all_to_all x1, starting transfers between devices, body(): gathered = lax.all_to_all(copies, TGT, 0, 0).reshape(features, group_rows)  11.9 us
    all_to_all x1, waiting for transfers between devices, body(): got = lax.all_to_all(sent, ('x',) + SRC, 0, 0)  10.2 us
    all_to_all x1, waiting for transfers between devices, body(): gathered = lax.all_to_all(copies, TGT, 0, 0).reshape(features, group_rows)  9.02 us
    all_to_all x1, starting transfers between devices, body(): got = lax.all_to_all(sent, ('x',) + SRC, 0, 0)  8.34 us
    pallas_call x3, Pallas kernels, call(): pl.pallas_call(kernel, out_shape=jax.ShapeDtypeStruct(shape, jnp.float32)...  3.4 us
    reduce_sum x1, other arithmetic, body(): tgt_scale = lax.rsqrt(jnp.sum(tgt_float * tgt_float, axis=1) + 1e-06)  2.07 us
    broadcast_in_dim x1, local copies, waits for them, and re-layouts, body(): copies = jnp.broadcast_to(sources.T[None], (Z * X,) + sources.T.shape)  1.58 us
  transfers between devices with their start and end apart: 2, of which 2 were waited for; matrix products, arithmetic and copies ran while one was open for 4% of the time, Pallas kernels for 0%

profile of v2, /device:TPU:1, one launch (start us, length us, event | category | flops | bytes accessed | tf_op | source)
XLA Modules:
  0.0 58.7 jit_solution(11451707382127768355)
XLA Ops:
  0.0 0.0 copy-start
  0.0 0.0 copy-start.3
  0.0 0.0 copy-start.1
  0.0 0.0 copy-start.2
  0.0 1.6 %broadcast_in_dim.2 = bf16[32,32,128]{2,1,0:T(8,128)(2,1)} broadcast(bf16[32,128]{1,0:T(8,128)(2,1)} %bitcast.17), dimensions={1,2} | broadcast | bytes 270336 | tf_op jit(solution)/shard_map/broadcast_in_dim | solution.py:111
  1.6 11.9 %all-to-all-start = ((bf16[32,32,128]{2,1,0:T(8,128)(2,1)}), bf16[32,32,128]{2,1,0:T(8,128)(2,1)S(1)}, u32[]{:S(2)}, u32[]{:S(2)}) async-start(bf16[32,32,128]{2,1,0:T(8,128)(2,1)} %broadcast_in_dim.2), calls=%async_computation | async-start | bytes 524288 | tf_op jit(solution)/shard_map/all_to_all | solution.py:112
  13.5 0.1 pad_add_fusion.1.place_ref
  13.6 2.1 %multiply_reduce_fusion = f32[1024]{0:T(1024)S(1)} fusion(bf16[1024,1024]{1,0:T(8,128)(2,1)} %tgt_ref.1), kind=kLoop, calls=%fused_computation | loop fusion | flops 3144704 | bytes 2101248 | tf_op jit(solution)/shard_map/reduce_sum | solution.py:114
  15.6 9.0 %all-to-all-done = bf16[32,32,128]{2,1,0:T(8,128)(2,1)S(1)} async-done(((bf16[32,32,128]{2,1,0:T(8,128)(2,1)}), bf16[32,32,128]{2,1,0:T(8,128)(2,1)S(1)}, u32[]{:S(2)}, u32[]{:S(2)}) %all-to-all-start) | async-done | bytes 262176 | tf_op jit(solution)/shard_map/all_to_all | solution.py:112
  24.7 0.0 copy-done
  24.7 0.0 copy-done.3
  24.7 0.0 copy-done.1
  24.7 0.0 copy-done.2
  24.7 2.1 %shard_map.55 = f32[32,24,128]{2,1,0:T(8,128)} custom-call(s32[2]{0:T(128)S(1)} %pad_add_fusion.1.place_ref, bf16[1024,128]{1,0:T(8,128)(2,1)S(1)} %bitcast.12, bf16[1024,1024]{1,0:T(8,128)(2,1)S(1)} %copy-done, f32[8,128]{1,0:T(8,128)S(1)} %rsqrt_bitcast_fusion.scale_ref, s32[16,1024]{1,0:T(8,128)S(1)} %bitcast.13, s32[8,128]{1,0:T(8,128)S(1)} %bitcast.16, ...), custom_call_target="tpu_custom_call" | custom-call | tf_op jit(solution)/shard_map/pallas_call | solution.py:95
  26.8 8.3 %all-to-all-start.1 = ((f32[32,24,128]{2,1,0:T(8,128)}), f32[32,24,128]{2,1,0:T(8,128)S(1)}, u32[]{:S(2)}, u32[]{:S(2)}) async-start(f32[32,24,128]{2,1,0:T(8,128)} %shard_map.55), calls=%async_computation.1 | async-start | bytes 786432 | tf_op jit(solution)/shard_map/all_to_all | solution.py:120
  35.1 0.1 pad_add_fusion.place_ref
  35.2 10.2 %all-to-all-done.1.got_ref = f32[32,24,128]{2,1,0:T(8,128)S(1)} async-done(((f32[32,24,128]{2,1,0:T(8,128)}), f32[32,24,128]{2,1,0:T(8,128)S(1)}, u32[]{:S(2)}, u32[]{:S(2)}) %all-to-all-start.1) | async-done | bytes 393248 | tf_op jit(solution)/shard_map/all_to_all | solution.py:120
  45.4 0.7 %shard_map.56 = f32[8,32,128]{2,1,0:T(8,128)S(1)} custom-call(s32[2]{0:T(128)S(1)} %pad_add_fusion.place_ref, f32[32,24,128]{2,1,0:T(8,128)S(1)} %all-to-all-done.1.got_ref, s32[16,128]{1,0:T(8,128)S(1)} %bitcast.15), custom_call_target="tpu_custom_call" | custom-call | tf_op jit(solution)/shard_map/pallas_call | solution.py:95
  46.1 12.0 %all_to_all.15.got_ref = f32[8,32,128]{2,1,0:T(8,128)S(1)} all-to-all(f32[8,32,128]{2,1,0:T(8,128)S(1)} %shard_map.56), channel_id=1, replica_groups=mesh['z'=8,'x'=4,'y'=4,'core'=2] {'z'}, dimensions={0} | all-to-all | bytes 262144 | tf_op jit(solution)/shard_map/all_to_all | solution.py:123
  58.1 0.6 %shard_map.57 = f32[16,128]{1,0:T(8,128)} custom-call(f32[8,32,128]{2,1,0:T(8,128)S(1)} %all_to_all.15.got_ref), custom_call_target="tpu_custom_call" | custom-call | tf_op jit(solution)/shard_map/pallas_call | solution.py:95
  (1 shorter events, 0.0 us)
Async XLA Ops:
  0.0 24.7 %copy-start = (bf16[1024,1024]{1,0:T(8,128)(2,1)S(1)}, bf16[1024,1024]{1,0:T(8,128)(2,1)}, u32[]{:S(2)}) copy-start(bf16[1024,1024]{1,0:T(8,128)(2,1)} %tgt_ref.1) | copy-start | bytes 6291460
  0.0 24.7 %copy-start.3 = (s32[1024]{0:T(1024)S(1)}, s32[1024]{0:T(1024)}, u32[]{:S(2)}) copy-start(s32[1024]{0:T(1024)} %param.9) | copy-start | bytes 12292
  0.0 24.7 %copy-start.1 = (s32[1024,16]{0,1:T(8,128)S(1)}, s32[1024,16]{0,1:T(8,128)}, u32[]{:S(2)}) copy-start(s32[1024,16]{0,1:T(8,128)} %param.8) | copy-start | bytes 196612
  0.0 24.7 %copy-start.2 = (s32[128,16]{0,1:T(8,128)S(1)}, s32[128,16]{0,1:T(8,128)}, u32[]{:S(2)}) copy-start(s32[128,16]{0,1:T(8,128)} %param.7) | copy-start | bytes 24580
  1.6 23.1 %all-to-all-start = ((bf16[32,32,128]{2,1,0:T(8,128)(2,1)}), bf16[32,32,128]{2,1,0:T(8,128)(2,1)S(1)}, u32[]{:S(2)}, u32[]{:S(2)}) async-start(bf16[32,32,128]{2,1,0:T(8,128)(2,1)} %broadcast_in_dim.2), calls=%async_computation | async-start | bytes 524288 | tf_op jit(solution)/shard_map/all_to_all | solution.py:112
  26.8 18.6 %all-to-all-start.1 = ((f32[32,24,128]{2,1,0:T(8,128)}), f32[32,24,128]{2,1,0:T(8,128)S(1)}, u32[]{:S(2)}, u32[]{:S(2)}) async-start(f32[32,24,128]{2,1,0:T(8,128)} %shard_map.55), calls=%async_computation.1 | async-start | bytes 786432 | tf_op jit(solution)/shard_map/all_to_all | solution.py:120

commit v3 on v2

v3 whole, which is shorter than its diff:
```python
import jax
import jax.numpy as jnp
from jax import lax
from jax.experimental import pallas as pl
from jax.experimental.pallas import tpu as pltpu
from jax.sharding import Mesh, PartitionSpec as P

Z, X, Y, CORE = 8, 4, 4, 2
TGT = ("z", "x")
SRC = ("y", "core")
LANES = 128
VMEM_BYTES = 24 * 1024 * 1024


def take_rows(rows, index):
    return jnp.take_along_axis(rows, index, axis=0)


def take_lanes(rows, index):
    return jnp.take_along_axis(rows, index, axis=1)


def pick_from_tiles(block, index, first_row, picked):
    tile, row = index >> 3, index & 7
    for i in range(block.shape[0] // 8):
        match = tile == (first_row // 8 + i)
        rows = block[8 * i : 8 * i + 8, :]
        picked = [
            jnp.where(match[8 * h : 8 * h + 8], take_rows(rows, row[8 * h : 8 * h + 8]), picked[h])
            for h in range(len(picked))
        ]
    return picked


def pick_from_table(table, index):
    high, low = index >> 7, index & 127
    picked = [jnp.zeros((8, LANES), jnp.float32)] * 2
    for i in range(table.shape[0]):
        row = jnp.broadcast_to(table[i : i + 1, :], (8, LANES))
        picked = [
            jnp.where(high[8 * h : 8 * h + 8] == i, take_lanes(row, low[8 * h : 8 * h + 8]), picked[h])
            for h in range(2)
        ]
    return jnp.concatenate(picked, axis=0)


def score_kernel(src_ref, tgt_ref, bwd_ref, len_ref, fwd_ref, out_ref):
    fwd_local = fwd_ref[...] - lax.axis_index(TGT) * tgt_ref.shape[0]
    first_src = lax.axis_index(SRC) * LANES
    src = src_ref[...]
    src_float = src.astype(jnp.float32)
    src_scale = lax.rsqrt(jnp.sum(src_float * src_float, axis=0, keepdims=True) + 1e-06)
    slot = lax.broadcasted_iota(jnp.int32, (16, LANES), 0)
    cos = [jnp.zeros((8, LANES), jnp.float32)] * 2
    back, scales = [], []
    for c in range(tgt_ref.shape[0] // LANES):
        lanes = slice(LANES * c, LANES * c + LANES)
        rows = tgt_ref[lanes, :]
        tgt_float = rows.astype(jnp.float32)
        squares = tgt_float * tgt_float
        part = squares[:, :LANES]
        for f in range(LANES, squares.shape[1], LANES):
            part = part + squares[:, f : f + LANES]
        tgt_scale = lax.rsqrt(jnp.sum(part.T, axis=0, keepdims=True) + 1e-06)
        scales.append(tgt_scale)
        block = jnp.dot(rows, src, preferred_element_type=jnp.float32) * src_scale
        cos = pick_from_tiles(block, fwd_local, LANES * c, cos)
        bwd_local = bwd_ref[:, lanes] - first_src
        zero = [jnp.zeros((8, LANES), jnp.float32)] * 2
        sims = jnp.concatenate(pick_from_tiles(block.T, bwd_local, 0, zero), axis=0)
        length = len_ref[c : c + 1, :]
        total = jnp.sum(jnp.where(slot < length, sims, 0.0), axis=0, keepdims=True)
        back.append(total * tgt_scale / length.astype(jnp.float32))
    cos = jnp.concatenate(cos, axis=0) * pick_from_table(jnp.concatenate(scales, axis=0), fwd_local)
    sent = jnp.concatenate(back + [cos], axis=0)
    for d in range(out_ref.shape[0]):
        out_ref[d] = sent


def mean_kernel(got_ref, fwd_ref, out_ref):
    group = lax.axis_index(SRC)
    first_tgt = lax.axis_index("z") * (X * 8 * LANES)
    groups = got_ref.shape[0] // X
    table, cos = [], jnp.zeros((16, LANES), jnp.float32)
    for x in range(X):
        total = got_ref[x * groups, :8, :]
        for g in range(1, groups):
            total = total + got_ref[x * groups + g, :8, :]
        table.append(total)
        cos = cos + got_ref[x * groups + group, 8:, :]
    bwd = pick_from_table(jnp.concatenate(table, axis=0), fwd_ref[...] - first_tgt)
    for d in range(out_ref.shape[0]):
        out_ref[d, :16, :] = cos
        out_ref[d, 16:, :] = bwd


def margin_kernel(got_ref, out_ref):
    total = jnp.sum(got_ref[...], axis=0)
    cos, bwd = total[:16], total[16:]
    fwd_mean = jnp.mean(cos, axis=0, keepdims=True)
    out_ref[...] = cos / ((fwd_mean + bwd) * 0.5)


def call(kernel, shape, *args):
    return pl.pallas_call(
        kernel,
        out_shape=jax.ShapeDtypeStruct(shape, jnp.float32),
        in_specs=[pl.BlockSpec(memory_space=pltpu.VMEM)] * len(args),
        out_specs=pl.BlockSpec(memory_space=pltpu.VMEM),
        compiler_params=pltpu.CompilerParams(vmem_limit_bytes=VMEM_BYTES),
    )(*args)


def body(sources, targets, fwd_idx, bwd_idx, bwd_len):
    features = targets.shape[1]
    group_rows, neighbours = fwd_idx.shape
    fwd = fwd_idx.T
    copies = jnp.broadcast_to(sources.T[None], (Z * X,) + sources.T.shape)
    gathered = lax.all_to_all(copies, TGT, 0, 0).reshape(features, group_rows)
    sent = call(
        score_kernel, (X * Y * CORE, 24, LANES), gathered, targets, bwd_idx.T, bwd_len.reshape(-1, LANES), fwd
    )
    got = lax.all_to_all(sent, ("x",) + SRC, 0, 0)
    sent = call(mean_kernel, (Z, 32, LANES), got, fwd)
    got = lax.all_to_all(sent, "z", 0, 0)
    return call(margin_kernel, (neighbours, group_rows), got).T


def solution(mesh):
    grid = Mesh(mesh.devices.reshape(Z, X, Y, CORE), TGT + SRC)
    in_specs = (P(SRC, TGT), P(TGT, None), P(SRC, None), P(TGT, None), P(TGT))
    return jax.shard_map(body, mesh=grid, in_specs=in_specs, out_specs=P(SRC, None), check_vma=False)
```

time: 59.1 us -> 60.1 us (1.017)
  blocking collectives: 12 us -> 53.3 us
  starting transfers between devices: 20.2 us -> 0 us
  waiting for transfers between devices: 19.2 us -> 0 us
  local copies, waits for them, and re-layouts: 1.59 us -> 4.54 us
  other arithmetic: 2.22 us -> 0 us
  Pallas kernels: 3.4 us -> 1.84 us
    all_to_all x0 -> x2, blocking collectives: none -> 41.3 us  [the longest x1 22.9 us: body(): gathered = lax.all_to_all(copies, TGT, 0, 0).reshape(features, group_rows)]
    all_to_all x2 -> x0, starting transfers between devices: 20.2 us -> none  [the longest x1 11.9 us: body(): gathered = lax.all_to_all(copies, TGT, 0, 0).reshape(features, group_rows)]
    all_to_all x2 -> x0, waiting for transfers between devices: 19.2 us -> none  [the longest x1 10.2 us: body(): got = lax.all_to_all(sent, ('x',) + SRC, 0, 0)]
    unnamed x8, local copies, waits for them, and re-layouts: 0.02 us -> 3.81 us
    reduce_sum x1 -> x0, other arithmetic: 2.07 us -> none  [body(): tgt_scale = lax.rsqrt(jnp.sum(tgt_float * tgt_float, axis=1) + 1e-06)]
    pallas_call x3, Pallas kernels: 3.4 us -> 1.84 us  [call(): pl.pallas_call(kernel, out_shape=jax.ShapeDtypeStruct(shape, jnp.float32)...]
    broadcast_in_dim x1, local copies, waits for them, and re-layouts: 1.58 us -> 0.73 us  [body(): copies = jnp.broadcast_to(sources.T[None], (Z * X,) + sources.T.shape)]
  transfers between devices with their start and end apart: 2 -> 0, of which waited for: 2 -> 0; matrix products, arithmetic and copies ran while one was open for 4% -> 0% of each run, Pallas kernels for 0% -> 0%
where the time goes in v3:
time: 60.1 us; the launch traced here: 59.7 us
  blocking collectives  53.3 us (89%)
  local copies, waits for them, and re-layouts  4.54 us (8%)
  Pallas kernels  1.84 us (3%)
    all_to_all x1, blocking collectives, body(): gathered = lax.all_to_all(copies, TGT, 0, 0).reshape(features, group_rows)  22.9 us
    all_to_all x1, blocking collectives, body(): got = lax.all_to_all(sent, ('x',) + SRC, 0, 0)  18.4 us
    all_to_all x1, blocking collectives, body(): got = lax.all_to_all(sent, 'z', 0, 0)  12 us
    unnamed x8, local copies, waits for them, and re-layouts  3.81 us
    pallas_call x3, Pallas kernels, call(): pl.pallas_call(kernel, out_shape=jax.ShapeDtypeStruct(shape, jnp.float32)...  1.84 us

profile of v3, /device:TPU:1, one launch (start us, length us, event | category | flops | bytes accessed | tf_op | source)
XLA Modules:
  0.0 59.7 jit_solution(18177594716801305257)
XLA Ops:
  0.0 0.7 %broadcast_in_dim.2 = bf16[32,32,128]{2,1,0:T(8,128)(2,1)S(1)} broadcast(bf16[32,128]{1,0:T(8,128)(2,1)} %bitcast.11), dimensions={1,2} | broadcast | bytes 270336 | tf_op jit(solution)/shard_map/broadcast_in_dim | solution.py:118
  0.7 22.9 %all_to_all.15 = bf16[32,32,128]{2,1,0:T(8,128)(2,1)S(1)} all-to-all(bf16[32,32,128]{2,1,0:T(8,128)(2,1)S(1)} %broadcast_in_dim.2), channel_id=1, replica_groups=mesh['z'=8,'x'=4,'y'=4,'core'=2] {'z','x'}, dimensions={0} | all-to-all | bytes 524288 | tf_op jit(solution)/shard_map/all_to_all | solution.py:119
  23.6 0.0 copy-start
  23.6 1.6 %copy-done = bf16[1024,1024]{1,0:T(8,128)(2,1)S(1)} copy-done((bf16[1024,1024]{1,0:T(8,128)(2,1)S(1)}, bf16[1024,1024]{1,0:T(8,128)(2,1)}, u32[]{:S(2)}) %copy-start) | copy-done | bytes 2097176
  25.2 0.0 copy-start.1
  25.2 0.8 %copy-done.1 = s32[1024,16]{0,1:T(8,128)S(1)} copy-done((s32[1024,16]{0,1:T(8,128)S(1)}, s32[1024,16]{0,1:T(8,128)}, u32[]{:S(2)}) %copy-start.1) | copy-done | bytes 65560
  26.0 0.0 copy-start.2
  26.0 0.7 %copy-done.2 = s32[128,16]{0,1:T(8,128)S(1)} copy-done((s32[128,16]{0,1:T(8,128)S(1)}, s32[128,16]{0,1:T(8,128)}, u32[]{:S(2)}) %copy-start.2) | copy-done | bytes 8216
  26.7 0.0 copy-start.3
  26.7 0.7 %copy-done.3 = s32[1024]{0:T(1024)S(1)} copy-done((s32[1024]{0:T(1024)S(1)}, s32[1024]{0:T(1024)}, u32[]{:S(2)}) %copy-start.3) | copy-done | bytes 4120
  27.4 1.1 %shard_map.55 = f32[32,24,128]{2,1,0:T(8,128)S(1)} custom-call(bf16[1024,128]{1,0:T(8,128)(2,1)S(1)} %bitcast.6, bf16[1024,1024]{1,0:T(8,128)(2,1)S(1)} %copy-done, s32[16,1024]{1,0:T(8,128)S(1)} %bitcast.7, s32[8,128]{1,0:T(8,128)S(1)} %bitcast.10, s32[16,128]{1,0:T(8,128)S(1)} %bitcast.8), custom_call_target="tpu_custom_call" | custom-call | tf_op jit(solution)/shard_map/pallas_call | solution.py:105
  28.5 18.4 %all_to_all.16.got_ref = f32[32,24,128]{2,1,0:T(8,128)S(1)} all-to-all(f32[32,24,128]{2,1,0:T(8,128)S(1)} %shard_map.55), channel_id=1, replica_groups=mesh['z'=8,'x'=4,'y'=4,'core'=2] {'x','y','core'}, dimensions={0} | all-to-all | bytes 786432 | tf_op jit(solution)/shard_map/all_to_all | solution.py:123
  46.9 0.1 shard_map.56
  47.1 12.0 %all_to_all.17.got_ref = f32[8,32,128]{2,1,0:T(8,128)S(1)} all-to-all(f32[8,32,128]{2,1,0:T(8,128)S(1)} %shard_map.56), channel_id=1, replica_groups=mesh['z'=8,'x'=4,'y'=4,'core'=2] {'z'}, dimensions={0} | all-to-all | bytes 262144 | tf_op jit(solution)/shard_map/all_to_all | solution.py:125
  59.1 0.6 %shard_map.57 = f32[16,128]{1,0:T(8,128)} custom-call(f32[8,32,128]{2,1,0:T(8,128)S(1)} %all_to_all.17.got_ref), custom_call_target="tpu_custom_call" | custom-call | tf_op jit(solution)/shard_map/pallas_call | solution.py:105
Async XLA Ops:
  23.6 1.6 %copy-start = (bf16[1024,1024]{1,0:T(8,128)(2,1)S(1)}, bf16[1024,1024]{1,0:T(8,128)(2,1)}, u32[]{:S(2)}) copy-start(bf16[1024,1024]{1,0:T(8,128)(2,1)} %tgt_ref.1) | copy-start | bytes 6291460
  25.2 0.8 %copy-start.1 = (s32[1024,16]{0,1:T(8,128)S(1)}, s32[1024,16]{0,1:T(8,128)}, u32[]{:S(2)}) copy-start(s32[1024,16]{0,1:T(8,128)} %param.8) | copy-start | bytes 196612
  26.0 0.7 %copy-start.2 = (s32[128,16]{0,1:T(8,128)S(1)}, s32[128,16]{0,1:T(8,128)}, u32[]{:S(2)}) copy-start(s32[128,16]{0,1:T(8,128)} %param.7) | copy-start | bytes 24580
  26.7 0.7 %copy-start.3 = (s32[1024]{0:T(1024)S(1)}, s32[1024]{0:T(1024)}, u32[]{:S(2)}) copy-start(s32[1024]{0:T(1024)} %param.9) | copy-start | bytes 12292

commit v4 on v3

--- a/solution.py
+++ b/solution.py
@@ -44,12 +44,18 @@
     return jnp.concatenate(picked, axis=0)
 
 
-def score_kernel(src_ref, tgt_ref, bwd_ref, len_ref, fwd_ref, out_ref):
-    fwd_local = fwd_ref[...] - lax.axis_index(TGT) * tgt_ref.shape[0]
-    first_src = lax.axis_index(SRC) * LANES
+def score_kernel(src_ref, tgt_hbm, bwd_hbm, len_hbm, fwd_hbm, out_ref, fwd_ref, tgt_ref, bwd_ref, len_ref, sems):
+    pairs = ((tgt_hbm, tgt_ref), (bwd_hbm, bwd_ref), (len_hbm, len_ref), (fwd_hbm, fwd_ref))
+    loads = [pltpu.make_async_copy(hbm, ref, sems.at[i]) for i, (hbm, ref) in enumerate(pairs)]
+    for load in loads:
+        load.start()
     src = src_ref[...]
     src_float = src.astype(jnp.float32)
     src_scale = lax.rsqrt(jnp.sum(src_float * src_float, axis=0, keepdims=True) + 1e-06)
+    for load in loads:
+        load.wait()
+    fwd_local = fwd_ref[...] - lax.axis_index(TGT) * tgt_ref.shape[0]
+    first_src = lax.axis_index(SRC) * LANES
     slot = lax.broadcasted_iota(jnp.int32, (16, LANES), 0)
     cos = [jnp.zeros((8, LANES), jnp.float32)] * 2
     back, scales = [], []
@@ -101,12 +107,13 @@
     out_ref[...] = cos / ((fwd_mean + bwd) * 0.5)
 
 
-def call(kernel, shape, *args):
+def call(kernel, shapes, memory, *args, scratch=()):
     return pl.pallas_call(
         kernel,
-        out_shape=jax.ShapeDtypeStruct(shape, jnp.float32),
-        in_specs=[pl.BlockSpec(memory_space=pltpu.VMEM)] * len(args),
-        out_specs=pl.BlockSpec(memory_space=pltpu.VMEM),
+        out_shape=[jax.ShapeDtypeStruct(shape, dtype) for shape, dtype in shapes],
+        in_specs=[pl.BlockSpec(memory_space=space) for space in memory],
+        out_specs=[pl.BlockSpec(memory_space=pltpu.VMEM)] * len(shapes),
+        scratch_shapes=scratch,
         compiler_params=pltpu.CompilerParams(vmem_limit_bytes=VMEM_BYTES),
     )(*args)
 
@@ -114,16 +121,23 @@
 def body(sources, targets, fwd_idx, bwd_idx, bwd_len):
     features = targets.shape[1]
     group_rows, neighbours = fwd_idx.shape
-    fwd = fwd_idx.T
+    vmem, hbm = pltpu.VMEM, pltpu.HBM
     copies = jnp.broadcast_to(sources.T[None], (Z * X,) + sources.T.shape)
     gathered = lax.all_to_all(copies, TGT, 0, 0).reshape(features, group_rows)
-    sent = call(
-        score_kernel, (X * Y * CORE, 24, LANES), gathered, targets, bwd_idx.T, bwd_len.reshape(-1, LANES), fwd
+    inputs = (targets, bwd_idx.T, bwd_len.reshape(-1, LANES), fwd_idx.T)
+    inputs = [pltpu.with_memory_space_constraint(a, hbm) for a in inputs]
+    sent, fwd = call(
+        score_kernel,
+        [((X * Y * CORE, 24, LANES), jnp.float32), ((neighbours, group_rows), jnp.int32)],
+        [vmem] + [hbm] * 4,
+        gathered,
+        *inputs,
+        scratch=[vmem(a.shape, a.dtype) for a in inputs[:3]] + [pltpu.SemaphoreType.DMA((4,))],
     )
     got = lax.all_to_all(sent, ("x",) + SRC, 0, 0)
-    sent = call(mean_kernel, (Z, 32, LANES), got, fwd)
+    (sent,) = call(mean_kernel, [((Z, 32, LANES), jnp.float32)], [vmem] * 2, got, fwd)
     got = lax.all_to_all(sent, "z", 0, 0)
-    return call(margin_kernel, (neighbours, group_rows), got).T
+    return call(margin_kernel, [((neighbours, group_rows), jnp.float32)], [vmem], got)[0].T
 
 
 def solution(mesh):

time: 60.1 us -> 57.7 us (0.960)
  local copies, waits for them, and re-layouts: 4.54 us -> 0.73 us
  Pallas kernels: 1.84 us -> 3.45 us
    unnamed x8 -> x0, local copies, waits for them, and re-layouts: 3.81 us -> none
    pallas_call x3, Pallas kernels: 1.84 us -> 3.45 us  [call(): pl.pallas_call(kernel, out_shape=[jax.ShapeDtypeStruct(shape, dtype) for...]
where the time goes in v4:
time: 57.7 us; the launch traced here: 57.5 us
  blocking collectives  53.3 us (92%)
  Pallas kernels  3.45 us (6%)
  local copies, waits for them, and re-layouts  0.73 us (1%)
    all_to_all x1, blocking collectives, body(): gathered = lax.all_to_all(copies, TGT, 0, 0).reshape(features, group_rows)  22.9 us
    all_to_all x1, blocking collectives, body(): got = lax.all_to_all(sent, ('x',) + SRC, 0, 0)  18.4 us
    all_to_all x1, blocking collectives, body(): got = lax.all_to_all(sent, 'z', 0, 0)  12 us
    pallas_call x3, Pallas kernels, call(): pl.pallas_call(kernel, out_shape=[jax.ShapeDtypeStruct(shape, dtype) for...  3.45 us

profile of v4, /device:TPU:1, one launch (start us, length us, event | category | flops | bytes accessed | tf_op | source)
XLA Modules:
  0.0 57.5 jit_solution(17398712045789679355)
XLA Ops:
  0.0 0.7 %broadcast_in_dim.2 = bf16[32,32,128]{2,1,0:T(8,128)(2,1)S(1)} broadcast(bf16[32,128]{1,0:T(8,128)(2,1)} %bitcast.9), dimensions={1,2} | broadcast | bytes 270336 | tf_op jit(solution)/shard_map/broadcast_in_dim | solution.py:125
  0.7 22.9 %all_to_all.15 = bf16[32,32,128]{2,1,0:T(8,128)(2,1)S(1)} all-to-all(bf16[32,32,128]{2,1,0:T(8,128)(2,1)S(1)} %broadcast_in_dim.2), channel_id=1, replica_groups=mesh['z'=8,'x'=4,'y'=4,'core'=2] {'z','x'}, dimensions={0} | all-to-all | bytes 524288 | tf_op jit(solution)/shard_map/all_to_all | solution.py:126
  23.6 2.7 %shard_map.55 = (f32[32,24,128]{2,1,0:T(8,128)S(1)}, s32[16,128]{1,0:T(8,128)S(1)}) custom-call(bf16[1024,128]{1,0:T(8,128)(2,1)S(1)} %bitcast.6, bf16[1024,1024]{1,0:T(8,128)(2,1)} %tgt_hbm.1, s32[16,1024]{1,0:T(8,128)} %bitcast.7, s32[8,128]{1,0:T(8,128)} %bitcast.10, s32[16,128]{1,0:T(8,128)} %bitcast.8), custom_call_target="tpu_custom_call" | custom-call | tf_op jit(solution)/shard_map/pallas_call | solution.py:111
  26.3 18.4 %all_to_all.16.got_ref = f32[32,24,128]{2,1,0:T(8,128)S(1)} all-to-all(f32[32,24,128]{2,1,0:T(8,128)S(1)} %get-tuple-element.7), channel_id=1, replica_groups=mesh['z'=8,'x'=4,'y'=4,'core'=2] {'x','y','core'}, dimensions={0} | all-to-all | bytes 786432 | tf_op jit(solution)/shard_map/all_to_all | solution.py:137
  44.7 0.1 shard_map.56
  44.9 12.0 %all_to_all.17.got_ref = f32[8,32,128]{2,1,0:T(8,128)S(1)} all-to-all(f32[8,32,128]{2,1,0:T(8,128)S(1)} %shard_map.56), channel_id=1, replica_groups=mesh['z'=8,'x'=4,'y'=4,'core'=2] {'z'}, dimensions={0} | all-to-all | bytes 262144 | tf_op jit(solution)/shard_map/all_to_all | solution.py:139
  56.8 0.6 %shard_map.57 = f32[16,128]{1,0:T(8,128)} custom-call(f32[8,32,128]{2,1,0:T(8,128)S(1)} %all_to_all.17.got_ref), custom_call_target="tpu_custom_call" | custom-call | tf_op jit(solution)/shard_map/pallas_call | solution.py:111

commit v5 on v3

v5 whole, which is shorter than its diff:
```python
import jax
import jax.numpy as jnp
from jax import lax
from jax.experimental import pallas as pl
from jax.experimental.pallas import tpu as pltpu
from jax.sharding import Mesh, PartitionSpec as P

BITS = ("z2", "z1", "z0", "x1", "x0", "y1", "y0", "core")
Z_BITS, X_BITS, Y_BITS = BITS[:3], BITS[3:5], BITS[5:7]
TGT = Z_BITS + X_BITS
SRC = BITS[5:]
Z, X, GROUPS = 8, 4, 8
GATHER = ("x1", "x0", "z2", "z1", "z0")
SUM = ("x1", "x0", "y1", "y0")
SPREAD = ("z0", "z1", "z2")
LANES = 128
VMEM_BYTES = 24 * 1024 * 1024


def slot(order, axes, index):
    at = 0
    for n, axis in enumerate(reversed(axes)):
        bit = index >> n & 1
        at = at + bit * (1 << (len(order) - 1 - order.index(axis)))
    return at


def take_rows(rows, index):
    return jnp.take_along_axis(rows, index, axis=0)


def take_lanes(rows, index):
    return jnp.take_along_axis(rows, index, axis=1)


def pick_from_tiles(block, index, first_row, picked):
    tile, row = index >> 3, index & 7
    for i in range(block.shape[0] // 8):
        match = tile == (first_row // 8 + i)
        rows = block[8 * i : 8 * i + 8, :]
        picked = [
            jnp.where(match[8 * h : 8 * h + 8], take_rows(rows, row[8 * h : 8 * h + 8]), picked[h])
            for h in range(len(picked))
        ]
    return picked


def pick_from_table(table, index):
    high, low = index >> 7, index & 127
    picked = [jnp.zeros((8, LANES), jnp.float32)] * 2
    for i in range(table.shape[0]):
        row = jnp.broadcast_to(table[i : i + 1, :], (8, LANES))
        picked = [
            jnp.where(high[8 * h : 8 * h + 8] == i, take_lanes(row, low[8 * h : 8 * h + 8]), picked[h])
            for h in range(2)
        ]
    return jnp.concatenate(picked, axis=0)


def score_kernel(src_ref, tgt_ref, scale_ref, bwd_ref, len_ref, fwd_ref, out_ref):
    src = jnp.concatenate([src_ref[slot(GATHER, TGT, t)] for t in range(Z * X)], axis=0)
    src_float = src.astype(jnp.float32)
    src_scale = lax.rsqrt(jnp.sum(src_float * src_float, axis=0, keepdims=True) + 1e-06)
    fwd_local = fwd_ref[...] - lax.axis_index(TGT) * tgt_ref.shape[0]
    first_src = lax.axis_index(SRC) * LANES
    neighbour = lax.broadcasted_iota(jnp.int32, (16, LANES), 0)
    cos = [jnp.zeros((8, LANES), jnp.float32)] * 2
    tgt_scale, back = scale_ref[...], []
    for c in range(tgt_ref.shape[0] // LANES):
        lanes = slice(LANES * c, LANES * c + LANES)
        block = jnp.dot(tgt_ref[lanes, :], src, preferred_element_type=jnp.float32) * src_scale
        cos = pick_from_tiles(block, fwd_local, LANES * c, cos)
        zero = [jnp.zeros((8, LANES), jnp.float32)] * 2
        sims = jnp.concatenate(pick_from_tiles(block.T, bwd_ref[:, lanes] - first_src, 0, zero), axis=0)
        length = len_ref[c : c + 1, :]
        total = jnp.sum(jnp.where(neighbour < length, sims, 0.0), axis=0, keepdims=True)
        back.append(total * tgt_scale[c : c + 1, :] / length.astype(jnp.float32))
    cos = jnp.concatenate(cos, axis=0) * pick_from_table(tgt_scale, fwd_local)
    out_ref[...] = jnp.concatenate(back + [cos], axis=0)


def join_kernel(own_ref, other_ref, out_ref):
    total = own_ref[:8, :] + other_ref[...]
    for d in range(out_ref.shape[0]):
        out_ref[d, :8, :] = total
        out_ref[d, 8:, :] = own_ref[8:, :]


def mean_kernel(got_ref, fwd_ref, out_ref):
    group = slot(SUM, Y_BITS, lax.axis_index(Y_BITS))
    first_tgt = lax.axis_index(Z_BITS) * (X * 8 * LANES)
    table, cos = [], jnp.zeros((16, LANES), jnp.float32)
    for x in range(X):
        at = slot(SUM, X_BITS, x)
        total = got_ref[at, :8, :]
        for g in range(1, GROUPS // 2):
            total = total + got_ref[at + slot(SUM, Y_BITS, g), :8, :]
        table.append(total)
        cos = cos + got_ref[at + group, 8:, :]
    bwd = pick_from_table(jnp.concatenate(table, axis=0), fwd_ref[...] - first_tgt)
    for d in range(out_ref.shape[0]):
        out_ref[d, :16, :] = cos
        out_ref[d, 16:, :] = bwd


def margin_kernel(got_ref, out_ref):
    total = jnp.sum(got_ref[...], axis=0)
    cos, bwd = total[:16], total[16:]
    fwd_mean = jnp.mean(cos, axis=0, keepdims=True)
    out_ref[...] = cos / ((fwd_mean + bwd) * 0.5)


def call(kernel, shape, *args):
    return pl.pallas_call(
        kernel,
        out_shape=jax.ShapeDtypeStruct(shape, jnp.float32),
        in_specs=[pl.BlockSpec(memory_space=pltpu.VMEM)] * len(args),
        out_specs=pl.BlockSpec(memory_space=pltpu.VMEM),
        compiler_params=pltpu.CompilerParams(vmem_limit_bytes=VMEM_BYTES),
    )(*args)


def body(sources, targets, fwd_idx, bwd_idx, bwd_len):
    group_rows, neighbours = fwd_idx.shape
    fwd = fwd_idx.T
    copies = jnp.broadcast_to(sources.T[None], (Z * X,) + sources.T.shape)
    gathered = lax.all_to_all(copies, GATHER, 0, 0)
    tgt_float = targets.astype(jnp.float32)
    tgt_scale = lax.rsqrt(jnp.sum(tgt_float * tgt_float, axis=1) + 1e-06).reshape(-1, LANES)
    sent = call(
        score_kernel, (24, LANES),
        gathered, targets, tgt_scale, bwd_idx.T, bwd_len.reshape(-1, LANES), fwd,
    )
    other = lax.ppermute(sent[:8], "core", [(0, 1), (1, 0)])
    sent = call(join_kernel, (X * GROUPS // 2, 24, LANES), sent, other)
    got = lax.all_to_all(sent, SUM, 0, 0)
    sent = call(mean_kernel, (Z, 32, LANES), got, fwd)
    got = lax.all_to_all(sent, SPREAD, 0, 0)
    return call(margin_kernel, (neighbours, group_rows), got).T


def solution(mesh):
    grid = Mesh(mesh.devices.reshape((2,) * len(BITS)), BITS)
    in_specs = (P(SRC, TGT), P(TGT, None), P(SRC, None), P(TGT, None), P(TGT))
    return jax.shard_map(body, mesh=grid, in_specs=in_specs, out_specs=P(SRC, None), check_vma=False)
```

time: 60.1 us -> 52 us (0.87)
  the two profiles are of different devices: /device:TPU:1 before, /device:TPU:2 now
where the time goes in v5:
time: 52 us; the launch traced here: 51.3 us
  blocking collectives  23.9 us (46%)
  starting transfers between devices  11.7 us (22%)
  waiting for transfers between devices  10.3 us (20%)
  other arithmetic  2.07 us (4%)
  Pallas kernels  1.6 us (3%)
  local copies, waits for them, and re-layouts  1.59 us (3%)
    all_to_all x1, blocking collectives, body(): got = lax.all_to_all(sent, SUM, 0, 0)  13.2 us
    all_to_all x1, starting transfers between devices, body(): gathered = lax.all_to_all(copies, GATHER, 0, 0)  11.6 us
    all_to_all x1, blocking collectives, body(): got = lax.all_to_all(sent, SPREAD, 0, 0)  10.8 us
    all_to_all x1, waiting for transfers between devices, body(): gathered = lax.all_to_all(copies, GATHER, 0, 0)  9.2 us
    reduce_sum x1, other arithmetic, body(): jnp.sum(tgt_float * tgt_float, axis=1) + 1e-06  2.07 us
    pallas_call x4, Pallas kernels, call(): pl.pallas_call(kernel, out_shape=jax.ShapeDtypeStruct(shape, jnp.float32)...  1.6 us
    broadcast_in_dim x1, local copies, waits for them, and re-layouts, body(): copies = jnp.broadcast_to(sources.T[None], (Z * X,) + sources.T.shape)  1.57 us
    ppermute x1, waiting for transfers between devices, body(): other = lax.ppermute(sent[:8], 'core', [(0, 1), (1, 0)])  1.15 us
  transfers between devices with their start and end apart: 2, of which 2 were waited for; matrix products, arithmetic and copies ran while one was open for 4% of the time, Pallas kernels for 0%

profile of v5, /device:TPU:2, one launch (start us, length us, event | category | flops | bytes accessed | tf_op | source)
XLA Modules:
  0.0 51.3 jit_solution(2774525254538734083)
XLA Ops:
  0.0 0.0 copy-start
  0.0 0.0 copy-start.2
  0.0 0.0 copy-start.1
  0.0 0.0 copy-start.3
  0.0 1.6 %broadcast_in_dim.2 = bf16[32,32,128]{2,1,0:T(8,128)(2,1)} broadcast(bf16[32,128]{1,0:T(8,128)(2,1)} %bitcast.11), dimensions={1,2} | broadcast | bytes 270336 | tf_op jit(solution)/shard_map/broadcast_in_dim | solution.py:126
  1.6 11.6 %all-to-all-start = ((bf16[32,32,128]{2,1,0:T(8,128)(2,1)}), bf16[32,32,128]{2,1,0:T(8,128)(2,1)S(1)}, u32[]{:S(2)}, u32[]{:S(2)}) async-start(bf16[32,32,128]{2,1,0:T(8,128)(2,1)} %broadcast_in_dim.2), calls=%async_computation | async-start | bytes 524288 | tf_op jit(solution)/shard_map/all_to_all | solution.py:127
  13.2 2.1 %multiply_reduce_fusion = f32[1024]{0:T(1024)S(1)} fusion(bf16[1024,1024]{1,0:T(8,128)(2,1)} %tgt_ref.1), kind=kLoop, calls=%fused_computation | loop fusion | flops 3144704 | bytes 2101248 | tf_op jit(solution)/shard_map/reduce_sum | solution.py:129
  15.3 9.2 %all-to-all-done.src_ref = bf16[32,32,128]{2,1,0:T(8,128)(2,1)S(1)} async-done(((bf16[32,32,128]{2,1,0:T(8,128)(2,1)}), bf16[32,32,128]{2,1,0:T(8,128)(2,1)S(1)}, u32[]{:S(2)}, u32[]{:S(2)}) %all-to-all-start) | async-done | bytes 262176 | tf_op jit(solution)/shard_map/all_to_all | solution.py:127
  24.5 0.0 copy-done
  24.5 0.0 copy-done.2
  24.5 0.0 copy-done.1
  24.5 0.0 copy-done.3
  24.5 0.8 %shard_map.55.own_ref = f32[24,128]{1,0:T(8,128)S(1)} custom-call(bf16[32,32,128]{2,1,0:T(8,128)(2,1)S(1)} %all-to-all-done.src_ref, bf16[1024,1024]{1,0:T(8,128)(2,1)S(1)} %copy-done, f32[8,128]{1,0:T(8,128)S(1)} %rsqrt_bitcast_fusion.scale_ref, s32[16,1024]{1,0:T(8,128)S(1)} %bitcast.7, s32[8,128]{1,0:T(8,128)S(1)} %bitcast.10, s32[16,128]{1,0:T(8,128)S(1)} %bitcast.8), custom_call_target="tpu_custom_call" | custom-call | tf_op jit(solution)/shard_map/pallas_call | solution.py:114
  25.3 0.1 collective-permute-start
  25.4 1.2 %collective-permute-done.other_ref = f32[8,128]{1,0:T(8,128)S(1)} collective-permute-done((f32[8,128]{1,0:T(8,128)S(1)}, f32[8,128]{1,0:T(8,128)S(1)}, u32[]{:S(2)}, u32[]{:S(2)}) %collective-permute-start) | collective-permute-done | bytes 4128 | tf_op jit(solution)/shard_map/ppermute | solution.py:134
  26.6 13.2 %all_to_all.15.got_ref = f32[16,24,128]{2,1,0:T(8,128)S(1)} all-to-all(f32[16,24,128]{2,1,0:T(8,128)S(1)} %shard_map.56), channel_id=1, replica_groups=mesh['z2'=2,'z1'=2,'z0'=2,'x1'=2,'x0'=2,'y1'=2,'y0'=2,'core'=2] {'x1','x..., dimensions={0} | all-to-all | bytes 393216 | tf_op jit(solution)/shard_map/all_to_all | solution.py:136
  39.8 0.2 shard_map.57
  39.9 10.8 %all_to_all.16.got_ref = f32[8,32,128]{2,1,0:T(8,128)S(1)} all-to-all(f32[8,32,128]{2,1,0:T(8,128)S(1)} %shard_map.57), channel_id=1, replica_groups=mesh['z2'=2,'z1'=2,'z0'=2,'x1'=2,'x0'=2,'y1'=2,'y0'=2,'core'=2] {'z0','z..., dimensions={0} | all-to-all | bytes 262144 | tf_op jit(solution)/shard_map/all_to_all | solution.py:138
  50.7 0.6 %shard_map.58 = f32[16,128]{1,0:T(8,128)} custom-call(f32[8,32,128]{2,1,0:T(8,128)S(1)} %all_to_all.16.got_ref), custom_call_target="tpu_custom_call" | custom-call | tf_op jit(solution)/shard_map/pallas_call | solution.py:114
  (3 shorter events, 0.0 us)
Async XLA Ops:
  0.0 24.5 %copy-start = (bf16[1024,1024]{1,0:T(8,128)(2,1)S(1)}, bf16[1024,1024]{1,0:T(8,128)(2,1)}, u32[]{:S(2)}) copy-start(bf16[1024,1024]{1,0:T(8,128)(2,1)} %tgt_ref.1) | copy-start | bytes 6291460
  0.0 24.5 %copy-start.2 = (s32[128,16]{0,1:T(8,128)S(1)}, s32[128,16]{0,1:T(8,128)}, u32[]{:S(2)}) copy-start(s32[128,16]{0,1:T(8,128)} %param.7) | copy-start | bytes 24580
  0.0 24.5 %copy-start.1 = (s32[1024,16]{0,1:T(8,128)S(1)}, s32[1024,16]{0,1:T(8,128)}, u32[]{:S(2)}) copy-start(s32[1024,16]{0,1:T(8,128)} %param.8) | copy-start | bytes 196612
  0.0 24.5 %copy-start.3 = (s32[1024]{0:T(1024)S(1)}, s32[1024]{0:T(1024)}, u32[]{:S(2)}) copy-start(s32[1024]{0:T(1024)} %param.9) | copy-start | bytes 12292
  1.6 22.9 %all-to-all-start = ((bf16[32,32,128]{2,1,0:T(8,128)(2,1)}), bf16[32,32,128]{2,1,0:T(8,128)(2,1)S(1)}, u32[]{:S(2)}, u32[]{:S(2)}) async-start(bf16[32,32,128]{2,1,0:T(8,128)(2,1)} %broadcast_in_dim.2), calls=%async_computation | async-start | bytes 524288 | tf_op jit(solution)/shard_map/all_to_all | solution.py:127
  25.3 1.3 %collective-permute-start = (f32[8,128]{1,0:T(8,128)S(1)}, f32[8,128]{1,0:T(8,128)S(1)}, u32[]{:S(2)}, u32[]{:S(2)}) collective-permute-start(f32[8,128]{1,0:T(8,128)S(1)} %slice.4), channel_id=1, source_target_pairs={{0,1},{1,0},{2,3},{3,2},{4,5},{5,4},{6,7},{7,6},{8,9},{9,8},{10,11... | collective-permute-start | bytes 12296 | tf_op jit(solution)/shard_map/ppermute | solution.py:134

commit v6 on v5

--- a/solution.py
+++ b/solution.py
@@ -5,24 +5,14 @@
 from jax.experimental.pallas import tpu as pltpu
 from jax.sharding import Mesh, PartitionSpec as P
 
-BITS = ("z2", "z1", "z0", "x1", "x0", "y1", "y0", "core")
-Z_BITS, X_BITS, Y_BITS = BITS[:3], BITS[3:5], BITS[5:7]
-TGT = Z_BITS + X_BITS
-SRC = BITS[5:]
-Z, X, GROUPS = 8, 4, 8
-GATHER = ("x1", "x0", "z2", "z1", "z0")
-SUM = ("x1", "x0", "y1", "y0")
-SPREAD = ("z0", "z1", "z2")
+Z, X, Y, CORE = 8, 4, 4, 2
+TGT = ("z", "x")
+SRC = ("y", "core")
+GATHER = [((z + 4) % Z) * X + (x + 2) % X for x in range(X) for z in range(Z)]
+SUM = [((x + 2) % X) * Y + (y + 2) % Y for x in range(X) for y in range(Y)]
+SPREAD = [(z + 4) % Z for z in (0, 4, 2, 6, 1, 5, 3, 7)]
 LANES = 128
 VMEM_BYTES = 24 * 1024 * 1024
-
-
-def slot(order, axes, index):
-    at = 0
-    for n, axis in enumerate(reversed(axes)):
-        bit = index >> n & 1
-        at = at + bit * (1 << (len(order) - 1 - order.index(axis)))
-    return at
 
 
 def take_rows(rows, index):
@@ -58,7 +48,7 @@
 
 
 def score_kernel(src_ref, tgt_ref, scale_ref, bwd_ref, len_ref, fwd_ref, out_ref):
-    src = jnp.concatenate([src_ref[slot(GATHER, TGT, t)] for t in range(Z * X)], axis=0)
+    src = jnp.concatenate([src_ref[GATHER.index(t)] for t in range(Z * X)], axis=0)
     src_float = src.astype(jnp.float32)
     src_scale = lax.rsqrt(jnp.sum(src_float * src_float, axis=0, keepdims=True) + 1e-06)
     fwd_local = fwd_ref[...] - lax.axis_index(TGT) * tgt_ref.shape[0]
@@ -87,16 +77,17 @@
 
 
 def mean_kernel(got_ref, fwd_ref, out_ref):
-    group = slot(SUM, Y_BITS, lax.axis_index(Y_BITS))
-    first_tgt = lax.axis_index(Z_BITS) * (X * 8 * LANES)
+    y = lax.axis_index("y")
+    first_tgt = lax.axis_index("z") * (X * 8 * LANES)
     table, cos = [], jnp.zeros((16, LANES), jnp.float32)
     for x in range(X):
-        at = slot(SUM, X_BITS, x)
-        total = got_ref[at, :8, :]
-        for g in range(1, GROUPS // 2):
-            total = total + got_ref[at + slot(SUM, Y_BITS, g), :8, :]
+        parts = [SUM.index(x * Y + line) for line in range(Y)]
+        total = got_ref[parts[0], :8, :]
+        for at in parts[1:]:
+            total = total + got_ref[at, :8, :]
         table.append(total)
-        cos = cos + got_ref[at + group, 8:, :]
+        for line, at in enumerate(parts):
+            cos = cos + jnp.where(y == line, got_ref[at, 8:, :], 0.0)
     bwd = pick_from_table(jnp.concatenate(table, axis=0), fwd_ref[...] - first_tgt)
     for d in range(out_ref.shape[0]):
         out_ref[d, :16, :] = cos
@@ -120,11 +111,15 @@
     )(*args)
 
 
+def exchange(blocks, axes, order):
+    return lax.all_to_all(blocks, axes, 0, 0, axis_index_groups=[order])
+
+
 def body(sources, targets, fwd_idx, bwd_idx, bwd_len):
     group_rows, neighbours = fwd_idx.shape
     fwd = fwd_idx.T
     copies = jnp.broadcast_to(sources.T[None], (Z * X,) + sources.T.shape)
-    gathered = lax.all_to_all(copies, GATHER, 0, 0)
+    gathered = exchange(copies, TGT, GATHER)
     tgt_float = targets.astype(jnp.float32)
     tgt_scale = lax.rsqrt(jnp.sum(tgt_float * tgt_float, axis=1) + 1e-06).reshape(-1, LANES)
     sent = call(
@@ -132,14 +127,14 @@
         gathered, targets, tgt_scale, bwd_idx.T, bwd_len.reshape(-1, LANES), fwd,
     )
     other = lax.ppermute(sent[:8], "core", [(0, 1), (1, 0)])
-    sent = call(join_kernel, (X * GROUPS // 2, 24, LANES), sent, other)
-    got = lax.all_to_all(sent, SUM, 0, 0)
+    sent = call(join_kernel, (X * Y, 24, LANES), sent, other)
+    got = exchange(sent, ("x", "y"), SUM)
     sent = call(mean_kernel, (Z, 32, LANES), got, fwd)
-    got = lax.all_to_all(sent, SPREAD, 0, 0)
+    got = exchange(sent, "z", SPREAD)
     return call(margin_kernel, (neighbours, group_rows), got).T
 
 
 def solution(mesh):
-    grid = Mesh(mesh.devices.reshape((2,) * len(BITS)), BITS)
+    grid = Mesh(mesh.devices.reshape(Z, X, Y, CORE), TGT + SRC)
     in_specs = (P(SRC, TGT), P(TGT, None), P(SRC, None), P(TGT, None), P(TGT))
     return jax.shard_map(body, mesh=grid, in_specs=in_specs, out_specs=P(SRC, None), check_vma=False)

time: 52 us -> 47.4 us (0.912)
  waiting for transfers between devices: 10.3 us -> 6.65 us
  blocking collectives: 23.9 us -> 22.7 us
  starting transfers between devices: 11.7 us -> 12.3 us
    all_to_all x1, waiting for transfers between devices: 9.2 us -> 5.49 us  [exchange(): return lax.all_to_all(blocks, axes, 0, 0, axis_index_groups=[order])]
    all_to_all x2, blocking collectives: 23.9 us -> 22.7 us  [exchange(): return lax.all_to_all(blocks, axes, 0, 0, axis_index_groups=[order])]
    all_to_all x1, starting transfers between devices: 11.6 us -> 12.2 us  [exchange(): return lax.all_to_all(blocks, axes, 0, 0, axis_index_groups=[order])]
where the time goes in v6:
time: 47.4 us; the launch traced here: 46.9 us
  blocking collectives  22.7 us (48%)
  starting transfers between devices  12.3 us (26%)
  waiting for transfers between devices  6.65 us (14%)
  other arithmetic  2.07 us (4%)
  local copies, waits for them, and re-layouts  1.59 us (3%)
  Pallas kernels  1.59 us (3%)
    all_to_all x2, blocking collectives, exchange(): return lax.all_to_all(blocks, axes, 0, 0, axis_index_groups=[order])  22.7 us
    all_to_all x1, starting transfers between devices, exchange(): return lax.all_to_all(blocks, axes, 0, 0, axis_index_groups=[order])  12.2 us
    all_to_all x1, waiting for transfers between devices, exchange(): return lax.all_to_all(blocks, axes, 0, 0, axis_index_groups=[order])  5.49 us
    reduce_sum x1, other arithmetic, body(): jnp.sum(tgt_float * tgt_float, axis=1) + 1e-06  2.07 us
    pallas_call x4, Pallas kernels, call(): pl.pallas_call(kernel, out_shape=jax.ShapeDtypeStruct(shape, jnp.float32)...  1.59 us
    broadcast_in_dim x1, local copies, waits for them, and re-layouts, body(): copies = jnp.broadcast_to(sources.T[None], (Z * X,) + sources.T.shape)  1.57 us
    ppermute x1, waiting for transfers between devices, body(): other = lax.ppermute(sent[:8], 'core', [(0, 1), (1, 0)])  1.15 us
  transfers between devices with their start and end apart: 2, of which 2 were waited for; matrix products, arithmetic and copies ran while one was open for 4% of the time, Pallas kernels for 0%

profile of v6, /device:TPU:2, one launch (start us, length us, event | category | flops | bytes accessed | tf_op | source)
XLA Modules:
  0.0 46.9 jit_solution(11420736006591761793)
XLA Ops:
  0.0 0.0 copy-start
  0.0 0.0 copy-start.2
  0.0 0.0 copy-start.1
  0.0 0.0 copy-start.3
  0.0 1.6 %broadcast_in_dim.2 = bf16[32,32,128]{2,1,0:T(8,128)(2,1)} broadcast(bf16[32,128]{1,0:T(8,128)(2,1)} %bitcast.11), dimensions={1,2} | broadcast | bytes 270336 | tf_op jit(solution)/shard_map/broadcast_in_dim | solution.py:121
  1.6 12.2 %all-to-all-start = ((bf16[32,32,128]{2,1,0:T(8,128)(2,1)}), bf16[32,32,128]{2,1,0:T(8,128)(2,1)S(1)}, u32[]{:S(2)}, u32[]{:S(2)}) async-start(bf16[32,32,128]{2,1,0:T(8,128)(2,1)} %broadcast_in_dim.2), calls=%async_computation | async-start | bytes 524288 | tf_op jit(solution)/shard_map/all_to_all | solution.py:115
  13.8 2.1 %multiply_reduce_fusion = f32[1024]{0:T(1024)S(1)} fusion(bf16[1024,1024]{1,0:T(8,128)(2,1)} %tgt_ref.1), kind=kLoop, calls=%fused_computation | loop fusion | flops 3144704 | bytes 2101248 | tf_op jit(solution)/shard_map/reduce_sum | solution.py:124
  15.9 5.5 %all-to-all-done.src_ref = bf16[32,32,128]{2,1,0:T(8,128)(2,1)S(1)} async-done(((bf16[32,32,128]{2,1,0:T(8,128)(2,1)}), bf16[32,32,128]{2,1,0:T(8,128)(2,1)S(1)}, u32[]{:S(2)}, u32[]{:S(2)}) %all-to-all-start) | async-done | bytes 262176 | tf_op jit(solution)/shard_map/all_to_all | solution.py:115
  21.4 0.0 copy-done
  21.4 0.0 copy-done.2
  21.4 0.0 copy-done.1
  21.4 0.0 copy-done.3
  21.4 0.8 %shard_map.55.own_ref = f32[24,128]{1,0:T(8,128)S(1)} custom-call(bf16[32,32,128]{2,1,0:T(8,128)(2,1)S(1)} %all-to-all-done.src_ref, bf16[1024,1024]{1,0:T(8,128)(2,1)S(1)} %copy-done, f32[8,128]{1,0:T(8,128)S(1)} %rsqrt_bitcast_fusion.scale_ref, s32[16,1024]{1,0:T(8,128)S(1)} %bitcast.7, s32[8,128]{1,0:T(8,128)S(1)} %bitcast.10, s32[16,128]{1,0:T(8,128)S(1)} %bitcast.8), custom_call_target="tpu_custom_call" | custom-call | tf_op jit(solution)/shard_map/pallas_call | solution.py:105
  22.2 0.1 collective-permute-start
  22.3 1.2 %collective-permute-done.other_ref = f32[8,128]{1,0:T(8,128)S(1)} collective-permute-done((f32[8,128]{1,0:T(8,128)S(1)}, f32[8,128]{1,0:T(8,128)S(1)}, u32[]{:S(2)}, u32[]{:S(2)}) %collective-permute-start) | collective-permute-done | bytes 4128 | tf_op jit(solution)/shard_map/ppermute | solution.py:129
  23.5 11.8 %all_to_all.15.got_ref = f32[16,24,128]{2,1,0:T(8,128)S(1)} all-to-all(f32[16,24,128]{2,1,0:T(8,128)S(1)} %shard_map.56), channel_id=1, replica_groups={{20,22,16,18,28,30,24,26,4,6,0,2,12,14,8,10},{21,23,17,19,29,31,25,27,5..., dimensions={0} | all-to-all | bytes 393216 | tf_op jit(solution)/shard_map/all_to_all | solution.py:115
  35.3 0.1 shard_map.57
  35.5 10.8 %all_to_all.16.got_ref = f32[8,32,128]{2,1,0:T(8,128)S(1)} all-to-all(f32[8,32,128]{2,1,0:T(8,128)S(1)} %shard_map.57), channel_id=1, replica_groups={{128,0,192,64,160,32,224,96},{129,1,193,65,161,33,225,97},{130,2,194,66..., dimensions={0} | all-to-all | bytes 262144 | tf_op jit(solution)/shard_map/all_to_all | solution.py:115
  46.3 0.6 %shard_map.58 = f32[16,128]{1,0:T(8,128)} custom-call(f32[8,32,128]{2,1,0:T(8,128)S(1)} %all_to_all.16.got_ref), custom_call_target="tpu_custom_call" | custom-call | tf_op jit(solution)/shard_map/pallas_call | solution.py:105
  (3 shorter events, 0.0 us)
Async XLA Ops:
  0.0 21.4 %copy-start = (bf16[1024,1024]{1,0:T(8,128)(2,1)S(1)}, bf16[1024,1024]{1,0:T(8,128)(2,1)}, u32[]{:S(2)}) copy-start(bf16[1024,1024]{1,0:T(8,128)(2,1)} %tgt_ref.1) | copy-start | bytes 6291460
  0.0 21.4 %copy-start.2 = (s32[128,16]{0,1:T(8,128)S(1)}, s32[128,16]{0,1:T(8,128)}, u32[]{:S(2)}) copy-start(s32[128,16]{0,1:T(8,128)} %param.7) | copy-start | bytes 24580
  0.0 21.4 %copy-start.1 = (s32[1024,16]{0,1:T(8,128)S(1)}, s32[1024,16]{0,1:T(8,128)}, u32[]{:S(2)}) copy-start(s32[1024,16]{0,1:T(8,128)} %param.8) | copy-start | bytes 196612
  0.0 21.4 %copy-start.3 = (s32[1024]{0:T(1024)S(1)}, s32[1024]{0:T(1024)}, u32[]{:S(2)}) copy-start(s32[1024]{0:T(1024)} %param.9) | copy-start | bytes 12292
  1.6 19.8 %all-to-all-start = ((bf16[32,32,128]{2,1,0:T(8,128)(2,1)}), bf16[32,32,128]{2,1,0:T(8,128)(2,1)S(1)}, u32[]{:S(2)}, u32[]{:S(2)}) async-start(bf16[32,32,128]{2,1,0:T(8,128)(2,1)} %broadcast_in_dim.2), calls=%async_computation | async-start | bytes 524288 | tf_op jit(solution)/shard_map/all_to_all | solution.py:115
  22.2 1.3 %collective-permute-start = (f32[8,128]{1,0:T(8,128)S(1)}, f32[8,128]{1,0:T(8,128)S(1)}, u32[]{:S(2)}, u32[]{:S(2)}) collective-permute-start(f32[8,128]{1,0:T(8,128)S(1)} %slice.4), channel_id=1, source_target_pairs={{0,1},{1,0},{2,3},{3,2},{4,5},{5,4},{6,7},{7,6},{8,9},{9,8},{10,11... | collective-permute-start | bytes 12296 | tf_op jit(solution)/shard_map/ppermute | solution.py:129

commit v7 on v6

--- a/solution.py
+++ b/solution.py
@@ -8,9 +8,9 @@
 Z, X, Y, CORE = 8, 4, 4, 2
 TGT = ("z", "x")
 SRC = ("y", "core")
-GATHER = [((z + 4) % Z) * X + (x + 2) % X for x in range(X) for z in range(Z)]
+GATHER = [((z + 4) % Z) * X + (x + 2) % X for x in (0, 3, 2, 1) for z in range(Z)]
 SUM = [((x + 2) % X) * Y + (y + 2) % Y for x in range(X) for y in range(Y)]
-SPREAD = [(z + 4) % Z for z in (0, 4, 2, 6, 1, 5, 3, 7)]
+SPREAD = [(z + 4) % Z for z in (0, 4, 3, 5, 2, 6, 1, 7)]
 LANES = 128
 VMEM_BYTES = 24 * 1024 * 1024
 

time: 47.4 us -> 47 us (level)
  blocking collectives: 22.7 us -> 22 us
    all_to_all x2, blocking collectives: 22.7 us -> 22 us  [exchange(): return lax.all_to_all(blocks, axes, 0, 0, axis_index_groups=[order])]
where the time goes in v7:
time: 47 us; the launch traced here: 46.4 us
  blocking collectives  22 us (47%)
  starting transfers between devices  12.2 us (26%)
  waiting for transfers between devices  6.89 us (15%)
  other arithmetic  2.07 us (4%)
  local copies, waits for them, and re-layouts  1.59 us (3%)
  Pallas kernels  1.59 us (3%)
    all_to_all x2, blocking collectives, exchange(): return lax.all_to_all(blocks, axes, 0, 0, axis_index_groups=[order])  22 us
    all_to_all x1, starting transfers between devices, exchange(): return lax.all_to_all(blocks, axes, 0, 0, axis_index_groups=[order])  12.1 us
    all_to_all x1, waiting for transfers between devices, exchange(): return lax.all_to_all(blocks, axes, 0, 0, axis_index_groups=[order])  5.74 us
    reduce_sum x1, other arithmetic, body(): jnp.sum(tgt_float * tgt_float, axis=1) + 1e-06  2.07 us
    pallas_call x4, Pallas kernels, call(): pl.pallas_call(kernel, out_shape=jax.ShapeDtypeStruct(shape, jnp.float32)...  1.59 us
    broadcast_in_dim x1, local copies, waits for them, and re-layouts, body(): copies = jnp.broadcast_to(sources.T[None], (Z * X,) + sources.T.shape)  1.57 us
    ppermute x1, waiting for transfers between devices, body(): other = lax.ppermute(sent[:8], 'core', [(0, 1), (1, 0)])  1.15 us
  transfers between devices with their start and end apart: 2, of which 2 were waited for; matrix products, arithmetic and copies ran while one was open for 4% of the time, Pallas kernels for 0%

profile of v7, /device:TPU:2, one launch (start us, length us, event | category | flops | bytes accessed | tf_op | source)
XLA Modules:
  0.0 46.4 jit_solution(8825156574520637849)
XLA Ops:
  0.0 0.0 copy-start
  0.0 0.0 copy-start.2
  0.0 0.0 copy-start.1
  0.0 0.0 copy-start.3
  0.0 1.6 %broadcast_in_dim.2 = bf16[32,32,128]{2,1,0:T(8,128)(2,1)} broadcast(bf16[32,128]{1,0:T(8,128)(2,1)} %bitcast.11), dimensions={1,2} | broadcast | bytes 270336 | tf_op jit(solution)/shard_map/broadcast_in_dim | solution.py:121
  1.6 12.1 %all-to-all-start = ((bf16[32,32,128]{2,1,0:T(8,128)(2,1)}), bf16[32,32,128]{2,1,0:T(8,128)(2,1)S(1)}, u32[]{:S(2)}, u32[]{:S(2)}) async-start(bf16[32,32,128]{2,1,0:T(8,128)(2,1)} %broadcast_in_dim.2), calls=%async_computation | async-start | bytes 524288 | tf_op jit(solution)/shard_map/all_to_all | solution.py:115
  13.7 2.1 %multiply_reduce_fusion = f32[1024]{0:T(1024)S(1)} fusion(bf16[1024,1024]{1,0:T(8,128)(2,1)} %tgt_ref.1), kind=kLoop, calls=%fused_computation | loop fusion | flops 3144704 | bytes 2101248 | tf_op jit(solution)/shard_map/reduce_sum | solution.py:124
  15.8 5.7 %all-to-all-done.src_ref = bf16[32,32,128]{2,1,0:T(8,128)(2,1)S(1)} async-done(((bf16[32,32,128]{2,1,0:T(8,128)(2,1)}), bf16[32,32,128]{2,1,0:T(8,128)(2,1)S(1)}, u32[]{:S(2)}, u32[]{:S(2)}) %all-to-all-start) | async-done | bytes 262176 | tf_op jit(solution)/shard_map/all_to_all | solution.py:115
  21.5 0.0 copy-done
  21.5 0.0 copy-done.2
  21.5 0.0 copy-done.1
  21.5 0.0 copy-done.3
  21.6 0.8 %shard_map.55.own_ref = f32[24,128]{1,0:T(8,128)S(1)} custom-call(bf16[32,32,128]{2,1,0:T(8,128)(2,1)S(1)} %all-to-all-done.src_ref, bf16[1024,1024]{1,0:T(8,128)(2,1)S(1)} %copy-done, f32[8,128]{1,0:T(8,128)S(1)} %rsqrt_bitcast_fusion.scale_ref, s32[16,1024]{1,0:T(8,128)S(1)} %bitcast.7, s32[8,128]{1,0:T(8,128)S(1)} %bitcast.10, s32[16,128]{1,0:T(8,128)S(1)} %bitcast.8), custom_call_target="tpu_custom_call" | custom-call | tf_op jit(solution)/shard_map/pallas_call | solution.py:105
  22.4 0.1 collective-permute-start
  22.5 1.2 %collective-permute-done.other_ref = f32[8,128]{1,0:T(8,128)S(1)} collective-permute-done((f32[8,128]{1,0:T(8,128)S(1)}, f32[8,128]{1,0:T(8,128)S(1)}, u32[]{:S(2)}, u32[]{:S(2)}) %collective-permute-start) | collective-permute-done | bytes 4128 | tf_op jit(solution)/shard_map/ppermute | solution.py:129
  23.6 11.5 %all_to_all.15.got_ref = f32[16,24,128]{2,1,0:T(8,128)S(1)} all-to-all(f32[16,24,128]{2,1,0:T(8,128)S(1)} %shard_map.56), channel_id=1, replica_groups={{20,22,16,18,28,30,24,26,4,6,0,2,12,14,8,10},{21,23,17,19,29,31,25,27,5..., dimensions={0} | all-to-all | bytes 393216 | tf_op jit(solution)/shard_map/all_to_all | solution.py:115
  35.1 0.1 shard_map.57
  35.3 10.5 %all_to_all.16.got_ref = f32[8,32,128]{2,1,0:T(8,128)S(1)} all-to-all(f32[8,32,128]{2,1,0:T(8,128)S(1)} %shard_map.57), channel_id=1, replica_groups={{128,0,224,32,192,64,160,96},{129,1,225,33,193,65,161,97},{130,2,226,34..., dimensions={0} | all-to-all | bytes 262144 | tf_op jit(solution)/shard_map/all_to_all | solution.py:115
  45.8 0.6 %shard_map.58 = f32[16,128]{1,0:T(8,128)} custom-call(f32[8,32,128]{2,1,0:T(8,128)S(1)} %all_to_all.16.got_ref), custom_call_target="tpu_custom_call" | custom-call | tf_op jit(solution)/shard_map/pallas_call | solution.py:105
  (3 shorter events, 0.0 us)
Async XLA Ops:
  0.0 21.5 %copy-start = (bf16[1024,1024]{1,0:T(8,128)(2,1)S(1)}, bf16[1024,1024]{1,0:T(8,128)(2,1)}, u32[]{:S(2)}) copy-start(bf16[1024,1024]{1,0:T(8,128)(2,1)} %tgt_ref.1) | copy-start | bytes 6291460
  0.0 21.5 %copy-start.2 = (s32[128,16]{0,1:T(8,128)S(1)}, s32[128,16]{0,1:T(8,128)}, u32[]{:S(2)}) copy-start(s32[128,16]{0,1:T(8,128)} %param.7) | copy-start | bytes 24580
  0.0 21.5 %copy-start.1 = (s32[1024,16]{0,1:T(8,128)S(1)}, s32[1024,16]{0,1:T(8,128)}, u32[]{:S(2)}) copy-start(s32[1024,16]{0,1:T(8,128)} %param.8) | copy-start | bytes 196612
  0.0 21.5 %copy-start.3 = (s32[1024]{0:T(1024)S(1)}, s32[1024]{0:T(1024)}, u32[]{:S(2)}) copy-start(s32[1024]{0:T(1024)} %param.9) | copy-start | bytes 12292
  1.6 19.9 %all-to-all-start = ((bf16[32,32,128]{2,1,0:T(8,128)(2,1)}), bf16[32,32,128]{2,1,0:T(8,128)(2,1)S(1)}, u32[]{:S(2)}, u32[]{:S(2)}) async-start(bf16[32,32,128]{2,1,0:T(8,128)(2,1)} %broadcast_in_dim.2), calls=%async_computation | async-start | bytes 524288 | tf_op jit(solution)/shard_map/all_to_all | solution.py:115
  22.4 1.3 %collective-permute-start = (f32[8,128]{1,0:T(8,128)S(1)}, f32[8,128]{1,0:T(8,128)S(1)}, u32[]{:S(2)}, u32[]{:S(2)}) collective-permute-start(f32[8,128]{1,0:T(8,128)S(1)} %slice.4), channel_id=1, source_target_pairs={{0,1},{1,0},{2,3},{3,2},{4,5},{5,4},{6,7},{7,6},{8,9},{9,8},{10,11... | collective-permute-start | bytes 12296 | tf_op jit(solution)/shard_map/ppermute | solution.py:129

commit v8 on v7

--- a/solution.py
+++ b/solution.py
@@ -9,7 +9,7 @@
 TGT = ("z", "x")
 SRC = ("y", "core")
 GATHER = [((z + 4) % Z) * X + (x + 2) % X for x in (0, 3, 2, 1) for z in range(Z)]
-SUM = [((x + 2) % X) * Y + (y + 2) % Y for x in range(X) for y in range(Y)]
+SUM = [((x + 2) % X) * Y + (y + 2) % Y for x in (0, 3, 2, 1) for y in range(Y)]
 SPREAD = [(z + 4) % Z for z in (0, 4, 3, 5, 2, 6, 1, 7)]
 LANES = 128
 VMEM_BYTES = 24 * 1024 * 1024
@@ -47,33 +47,37 @@
     return jnp.concatenate(picked, axis=0)
 
 
-def score_kernel(src_ref, tgt_ref, scale_ref, bwd_ref, len_ref, fwd_ref, out_ref):
+def score_kernel(src_ref, tgt_ref, scale_ref, bwd_ref, len_ref, out_ref, block_ref):
     src = jnp.concatenate([src_ref[GATHER.index(t)] for t in range(Z * X)], axis=0)
     src_float = src.astype(jnp.float32)
     src_scale = lax.rsqrt(jnp.sum(src_float * src_float, axis=0, keepdims=True) + 1e-06)
-    fwd_local = fwd_ref[...] - lax.axis_index(TGT) * tgt_ref.shape[0]
     first_src = lax.axis_index(SRC) * LANES
     neighbour = lax.broadcasted_iota(jnp.int32, (16, LANES), 0)
-    cos = [jnp.zeros((8, LANES), jnp.float32)] * 2
     tgt_scale, back = scale_ref[...], []
     for c in range(tgt_ref.shape[0] // LANES):
         lanes = slice(LANES * c, LANES * c + LANES)
         block = jnp.dot(tgt_ref[lanes, :], src, preferred_element_type=jnp.float32) * src_scale
-        cos = pick_from_tiles(block, fwd_local, LANES * c, cos)
+        block_ref[lanes, :] = block
         zero = [jnp.zeros((8, LANES), jnp.float32)] * 2
         sims = jnp.concatenate(pick_from_tiles(block.T, bwd_ref[:, lanes] - first_src, 0, zero), axis=0)
         length = len_ref[c : c + 1, :]
         total = jnp.sum(jnp.where(neighbour < length, sims, 0.0), axis=0, keepdims=True)
         back.append(total * tgt_scale[c : c + 1, :] / length.astype(jnp.float32))
-    cos = jnp.concatenate(cos, axis=0) * pick_from_table(tgt_scale, fwd_local)
-    out_ref[...] = jnp.concatenate(back + [cos], axis=0)
+    out_ref[...] = jnp.concatenate(back, axis=0)
 
 
-def join_kernel(own_ref, other_ref, out_ref):
-    total = own_ref[:8, :] + other_ref[...]
+def forward_kernel(block_ref, scale_ref, fwd_ref, out_ref):
+    fwd_local = fwd_ref[...] - lax.axis_index(TGT) * block_ref.shape[0]
+    cos = [jnp.zeros((8, LANES), jnp.float32)] * 2
+    cos = jnp.concatenate(pick_from_tiles(block_ref[...], fwd_local, 0, cos), axis=0)
+    out_ref[...] = cos * pick_from_table(scale_ref[...], fwd_local)
+
+
+def join_kernel(own_ref, other_ref, cos_ref, out_ref):
+    total = own_ref[...] + other_ref[...]
     for d in range(out_ref.shape[0]):
         out_ref[d, :8, :] = total
-        out_ref[d, 8:, :] = own_ref[8:, :]
+        out_ref[d, 8:, :] = cos_ref[...]
 
 
 def mean_kernel(got_ref, fwd_ref, out_ref):
@@ -101,12 +105,12 @@
     out_ref[...] = cos / ((fwd_mean + bwd) * 0.5)
 
 
-def call(kernel, shape, *args):
+def call(kernel, shapes, *args):
     return pl.pallas_call(
         kernel,
-        out_shape=jax.ShapeDtypeStruct(shape, jnp.float32),
+        out_shape=[jax.ShapeDtypeStruct(shape, jnp.float32) for shape in shapes],
         in_specs=[pl.BlockSpec(memory_space=pltpu.VMEM)] * len(args),
-        out_specs=pl.BlockSpec(memory_space=pltpu.VMEM),
+        out_specs=[pl.BlockSpec(memory_space=pltpu.VMEM)] * len(shapes),
         compiler_params=pltpu.CompilerParams(vmem_limit_bytes=VMEM_BYTES),
     )(*args)
 
@@ -122,16 +126,17 @@
     gathered = exchange(copies, TGT, GATHER)
     tgt_float = targets.astype(jnp.float32)
     tgt_scale = lax.rsqrt(jnp.sum(tgt_float * tgt_float, axis=1) + 1e-06).reshape(-1, LANES)
-    sent = call(
-        score_kernel, (24, LANES),
-        gathered, targets, tgt_scale, bwd_idx.T, bwd_len.reshape(-1, LANES), fwd,
+    back, scores = call(
+        score_kernel, [(8, LANES), (targets.shape[0], group_rows)],
+        gathered, targets, tgt_scale, bwd_idx.T, bwd_len.reshape(-1, LANES),
     )
-    other = lax.ppermute(sent[:8], "core", [(0, 1), (1, 0)])
-    sent = call(join_kernel, (X * Y, 24, LANES), sent, other)
+    other = lax.ppermute(back, "core", [(0, 1), (1, 0)])
+    (cos,) = call(forward_kernel, [(neighbours, group_rows)], scores, tgt_scale, fwd)
+    (sent,) = call(join_kernel, [(X * Y, 24, LANES)], back, other, cos)
     got = exchange(sent, ("x", "y"), SUM)
-    sent = call(mean_kernel, (Z, 32, LANES), got, fwd)
+    (sent,) = call(mean_kernel, [(Z, 32, LANES)], got, fwd)
     got = exchange(sent, "z", SPREAD)
-    return call(margin_kernel, (neighbours, group_rows), got).T
+    return call(margin_kernel, [(neighbours, group_rows)], got)[0].T
 
 
 def solution(mesh):

time: 47 us -> 47 us (level)
    pallas_call x4 -> x5, Pallas kernels: 1.59 us -> 1.73 us  [call(): pl.pallas_call(kernel, out_shape=[jax.ShapeDtypeStruct(shape, jnp.float32...]
where the time goes in v8:
time: 47 us; the launch traced here: 46.7 us
  blocking collectives  22.3 us (47%)
  starting transfers between devices  12.2 us (26%)
  waiting for transfers between devices  6.7 us (14%)
  other arithmetic  2.08 us (4%)
  Pallas kernels  1.73 us (4%)
  local copies, waits for them, and re-layouts  1.6 us (3%)
    all_to_all x2, blocking collectives, exchange(): return lax.all_to_all(blocks, axes, 0, 0, axis_index_groups=[order])  22.3 us
    all_to_all x1, starting transfers between devices, exchange(): return lax.all_to_all(blocks, axes, 0, 0, axis_index_groups=[order])  12.1 us
    all_to_all x1, waiting for transfers between devices, exchange(): return lax.all_to_all(blocks, axes, 0, 0, axis_index_groups=[order])  5.72 us
    reduce_sum x1, other arithmetic, body(): jnp.sum(tgt_float * tgt_float, axis=1) + 1e-06  2.07 us
    pallas_call x5, Pallas kernels, call(): pl.pallas_call(kernel, out_shape=[jax.ShapeDtypeStruct(shape, jnp.float32...  1.73 us
    broadcast_in_dim x1, local copies, waits for them, and re-layouts, body(): copies = jnp.broadcast_to(sources.T[None], (Z * X,) + sources.T.shape)  1.58 us
    ppermute x1, waiting for transfers between devices, body(): other = lax.ppermute(back, 'core', [(0, 1), (1, 0)])  0.98 us
  transfers between devices with their start and end apart: 2, of which 2 were waited for; matrix products, arithmetic and copies ran while one was open for 4% of the time, Pallas kernels for 0%

profile of v8, /device:TPU:2, one launch (start us, length us, event | category | flops | bytes accessed | tf_op | source)
XLA Modules:
  0.0 46.7 jit_solution(8620694681382787216)
XLA Ops:
  0.0 0.0 copy-start
  0.0 0.0 copy-start.3
  0.0 0.0 copy-start.1
  0.0 1.6 %broadcast_in_dim.2 = bf16[32,32,128]{2,1,0:T(8,128)(2,1)} broadcast(bf16[32,128]{1,0:T(8,128)(2,1)} %bitcast.11), dimensions={1,2} | broadcast | bytes 270336 | tf_op jit(solution)/shard_map/broadcast_in_dim | solution.py:125
  1.6 12.1 %all-to-all-start = ((bf16[32,32,128]{2,1,0:T(8,128)(2,1)}), bf16[32,32,128]{2,1,0:T(8,128)(2,1)S(1)}, u32[]{:S(2)}, u32[]{:S(2)}) async-start(bf16[32,32,128]{2,1,0:T(8,128)(2,1)} %broadcast_in_dim.2), calls=%async_computation | async-start | bytes 524288 | tf_op jit(solution)/shard_map/all_to_all | solution.py:119
  13.7 0.0 copy-start.2
  13.7 2.1 %multiply_reduce_fusion = f32[1024]{0:T(1024)S(1)} fusion(bf16[1024,1024]{1,0:T(8,128)(2,1)} %tgt_ref.1), kind=kLoop, calls=%fused_computation | loop fusion | flops 3144704 | bytes 2101248 | tf_op jit(solution)/shard_map/reduce_sum | solution.py:128
  15.8 5.7 %all-to-all-done.src_ref = bf16[32,32,128]{2,1,0:T(8,128)(2,1)S(1)} async-done(((bf16[32,32,128]{2,1,0:T(8,128)(2,1)}), bf16[32,32,128]{2,1,0:T(8,128)(2,1)S(1)}, u32[]{:S(2)}, u32[]{:S(2)}) %all-to-all-start) | async-done | bytes 262176 | tf_op jit(solution)/shard_map/all_to_all | solution.py:119
  21.5 0.0 copy-done
  21.5 0.0 copy-done.3
  21.5 0.0 copy-done.1
  21.5 0.8 %shard_map.55 = (f32[8,128]{1,0:T(8,128)S(1)}, f32[1024,128]{1,0:T(8,128)S(1)}) custom-call(bf16[32,32,128]{2,1,0:T(8,128)(2,1)S(1)} %all-to-all-done.src_ref, bf16[1024,1024]{1,0:T(8,128)(2,1)S(1)} %copy-done, f32[8,128]{1,0:T(8,128)S(1)} %rsqrt_bitcast_fusion.scale_ref, s32[16,1024]{1,0:T(8,128)S(1)} %bitcast.7, s32[8,128]{1,0:T(8,128)S(1)} %bitcast.10), custom_call_target="tpu_custom_call" | custom-call | tf_op jit(solution)/shard_map/pallas_call | solution.py:109
  22.3 0.1 collective-permute-start
  22.4 0.0 copy-done.2
  22.4 0.2 shard_map.56.cos_ref
  22.6 1.0 %collective-permute-done.other_ref = f32[8,128]{1,0:T(8,128)S(1)} collective-permute-done((f32[8,128]{1,0:T(8,128)S(1)}, f32[8,128]{1,0:T(8,128)S(1)}, u32[]{:S(2)}, u32[]{:S(2)}) %collective-permute-start) | collective-permute-done | bytes 4128 | tf_op jit(solution)/shard_map/ppermute | solution.py:133
  23.6 11.7 %all_to_all.15.got_ref = f32[16,24,128]{2,1,0:T(8,128)S(1)} all-to-all(f32[16,24,128]{2,1,0:T(8,128)S(1)} %shard_map.57), channel_id=1, replica_groups={{20,22,16,18,12,14,8,10,4,6,0,2,28,30,24,26},{21,23,17,19,13,15,9,11,5,..., dimensions={0} | all-to-all | bytes 393216 | tf_op jit(solution)/shard_map/all_to_all | solution.py:119
  35.4 0.1 shard_map.58
  35.5 10.5 %all_to_all.16.got_ref = f32[8,32,128]{2,1,0:T(8,128)S(1)} all-to-all(f32[8,32,128]{2,1,0:T(8,128)S(1)} %shard_map.58), channel_id=1, replica_groups={{128,0,224,32,192,64,160,96},{129,1,225,33,193,65,161,97},{130,2,226,34..., dimensions={0} | all-to-all | bytes 262144 | tf_op jit(solution)/shard_map/all_to_all | solution.py:119
  46.0 0.6 %shard_map.59 = f32[16,128]{1,0:T(8,128)} custom-call(f32[8,32,128]{2,1,0:T(8,128)S(1)} %all_to_all.16.got_ref), custom_call_target="tpu_custom_call" | custom-call | tf_op jit(solution)/shard_map/pallas_call | solution.py:109
  (2 shorter events, 0.0 us)
Async XLA Ops:
  0.0 21.5 %copy-start = (bf16[1024,1024]{1,0:T(8,128)(2,1)S(1)}, bf16[1024,1024]{1,0:T(8,128)(2,1)}, u32[]{:S(2)}) copy-start(bf16[1024,1024]{1,0:T(8,128)(2,1)} %tgt_ref.1) | copy-start | bytes 6291460
  0.0 21.5 %copy-start.3 = (s32[1024]{0:T(1024)S(1)}, s32[1024]{0:T(1024)}, u32[]{:S(2)}) copy-start(s32[1024]{0:T(1024)} %param.9) | copy-start | bytes 12292
  0.0 21.5 %copy-start.1 = (s32[1024,16]{0,1:T(8,128)S(1)}, s32[1024,16]{0,1:T(8,128)}, u32[]{:S(2)}) copy-start(s32[1024,16]{0,1:T(8,128)} %param.8) | copy-start | bytes 196612
  1.6 19.9 %all-to-all-start = ((bf16[32,32,128]{2,1,0:T(8,128)(2,1)}), bf16[32,32,128]{2,1,0:T(8,128)(2,1)S(1)}, u32[]{:S(2)}, u32[]{:S(2)}) async-start(bf16[32,32,128]{2,1,0:T(8,128)(2,1)} %broadcast_in_dim.2), calls=%async_computation | async-start | bytes 524288 | tf_op jit(solution)/shard_map/all_to_all | solution.py:119
  13.7 8.7 %copy-start.2 = (s32[128,16]{0,1:T(8,128)S(1)}, s32[128,16]{0,1:T(8,128)}, u32[]{:S(2)}) copy-start(s32[128,16]{0,1:T(8,128)} %param.7) | copy-start | bytes 24580
  22.3 1.3 %collective-permute-start = (f32[8,128]{1,0:T(8,128)S(1)}, f32[8,128]{1,0:T(8,128)S(1)}, u32[]{:S(2)}, u32[]{:S(2)}) collective-permute-start(f32[8,128]{1,0:T(8,128)S(1)} %get-tuple-element.7.own_ref), channel_id=1, source_target_pairs={{0,1},{1,0},{2,3},{3,2},{4,5},{5,4},{6,7},{7,6},{8,9},{9,8},{10,11... | collective-permute-start | bytes 12296 | tf_op jit(solution)/shard_map/ppermute | solution.py:133

commit v9 on v7

--- a/solution.py
+++ b/solution.py
@@ -9,7 +9,7 @@
 TGT = ("z", "x")
 SRC = ("y", "core")
 GATHER = [((z + 4) % Z) * X + (x + 2) % X for x in (0, 3, 2, 1) for z in range(Z)]
-SUM = [((x + 2) % X) * Y + (y + 2) % Y for x in range(X) for y in range(Y)]
+SUM = [((x + 2) % X) * Y + (y + 2) % Y for x in (0, 3, 2, 1) for y in range(Y)]
 SPREAD = [(z + 4) % Z for z in (0, 4, 3, 5, 2, 6, 1, 7)]
 LANES = 128
 VMEM_BYTES = 24 * 1024 * 1024
@@ -45,6 +45,12 @@
             for h in range(2)
         ]
     return jnp.concatenate(picked, axis=0)
+
+
+def copy_kernel(src_ref, out_ref):
+    block = src_ref[...]
+    for d in range(out_ref.shape[0]):
+        out_ref[d] = block
 
 
 def score_kernel(src_ref, tgt_ref, scale_ref, bwd_ref, len_ref, fwd_ref, out_ref):
@@ -101,10 +107,10 @@
     out_ref[...] = cos / ((fwd_mean + bwd) * 0.5)
 
 
-def call(kernel, shape, *args):
+def call(kernel, shape, *args, dtype=jnp.float32):
     return pl.pallas_call(
         kernel,
-        out_shape=jax.ShapeDtypeStruct(shape, jnp.float32),
+        out_shape=jax.ShapeDtypeStruct(shape, dtype),
         in_specs=[pl.BlockSpec(memory_space=pltpu.VMEM)] * len(args),
         out_specs=pl.BlockSpec(memory_space=pltpu.VMEM),
         compiler_params=pltpu.CompilerParams(vmem_limit_bytes=VMEM_BYTES),
@@ -118,7 +124,7 @@
 def body(sources, targets, fwd_idx, bwd_idx, bwd_len):
     group_rows, neighbours = fwd_idx.shape
     fwd = fwd_idx.T
-    copies = jnp.broadcast_to(sources.T[None], (Z * X,) + sources.T.shape)
+    copies = call(copy_kernel, (Z * X,) + sources.T.shape, sources.T, dtype=sources.dtype)
     gathered = exchange(copies, TGT, GATHER)
     tgt_float = targets.astype(jnp.float32)
     tgt_scale = lax.rsqrt(jnp.sum(tgt_float * tgt_float, axis=1) + 1e-06).reshape(-1, LANES)

time: 47 us -> 47 us (level)
  local copies, waits for them, and re-layouts: 1.59 us -> 0.86 us
  Pallas kernels: 1.59 us -> 2.32 us
    broadcast_in_dim x1 -> x0, local copies, waits for them, and re-layouts: 1.57 us -> none  [body(): copies = jnp.broadcast_to(sources.T[None], (Z * X,) + sources.T.shape)]
    unnamed x8 -> x10, local copies, waits for them, and re-layouts: 0.02 us -> 0.85 us
    pallas_call x4 -> x5, Pallas kernels: 1.59 us -> 2.32 us  [call(): pl.pallas_call(kernel, out_shape=jax.ShapeDtypeStruct(shape, dtype), in_s...]
where the time goes in v9:
time: 47 us; the launch traced here: 46.7 us
  blocking collectives  22.3 us (47%)
  starting transfers between devices  12.2 us (26%)
  waiting for transfers between devices  6.89 us (15%)
  Pallas kernels  2.32 us (5%)
  other arithmetic  2.07 us (4%)
  local copies, waits for them, and re-layouts  0.86 us (2%)
    all_to_all x2, blocking collectives, exchange(): return lax.all_to_all(blocks, axes, 0, 0, axis_index_groups=[order])  22.3 us
    all_to_all x1, starting transfers between devices, exchange(): return lax.all_to_all(blocks, axes, 0, 0, axis_index_groups=[order])  12.1 us
    all_to_all x1, waiting for transfers between devices, exchange(): return lax.all_to_all(blocks, axes, 0, 0, axis_index_groups=[order])  5.74 us
    pallas_call x5, Pallas kernels, call(): pl.pallas_call(kernel, out_shape=jax.ShapeDtypeStruct(shape, dtype), in_s...  2.32 us
    reduce_sum x1, other arithmetic, body(): jnp.sum(tgt_float * tgt_float, axis=1) + 1e-06  2.07 us
    ppermute x1, waiting for transfers between devices, body(): other = lax.ppermute(sent[:8], 'core', [(0, 1), (1, 0)])  1.15 us
  transfers between devices with their start and end apart: 2, of which 2 were waited for; matrix products, arithmetic and copies ran while one was open for 4% of the time, Pallas kernels for 0%

profile of v9, /device:TPU:2, one launch (start us, length us, event | category | flops | bytes accessed | tf_op | source)
XLA Modules:
  0.0 46.7 jit_solution(11733968306135225210)
XLA Ops:
  0.0 0.0 copy-start
  0.0 0.0 copy-start.2
  0.0 0.0 copy-start.1
  0.0 0.0 copy-start.3
  0.0 0.8 %copy-done.3 = bf16[128,32]{0,1:T(8,128)(2,1)S(1)} copy-done((bf16[128,32]{0,1:T(8,128)(2,1)S(1)}, bf16[128,32]{0,1:T(8,128)(2,1)}, u32[]{:S(2)}) %copy-start.3) | copy-done | bytes 8216
  0.9 0.0 copy-start.4
  0.9 0.7 %shard_map.55 = bf16[32,32,128]{2,1,0:T(8,128)(2,1)} custom-call(bf16[32,128]{1,0:T(8,128)(2,1)S(1)} %bitcast.10), custom_call_target="tpu_custom_call" | custom-call | tf_op jit(solution)/shard_map/pallas_call | solution.py:111
  1.6 12.1 %all-to-all-start = ((bf16[32,32,128]{2,1,0:T(8,128)(2,1)}), bf16[32,32,128]{2,1,0:T(8,128)(2,1)S(1)}, u32[]{:S(2)}, u32[]{:S(2)}) async-start(bf16[32,32,128]{2,1,0:T(8,128)(2,1)} %shard_map.55), calls=%async_computation | async-start | bytes 524288 | tf_op jit(solution)/shard_map/all_to_all | solution.py:121
  13.7 2.1 %multiply_reduce_fusion = f32[1024]{0:T(1024)S(1)} fusion(bf16[1024,1024]{1,0:T(8,128)(2,1)} %tgt_ref.1), kind=kLoop, calls=%fused_computation | loop fusion | flops 3144704 | bytes 2101248 | tf_op jit(solution)/shard_map/reduce_sum | solution.py:130
  15.8 5.7 %all-to-all-done.src_ref = bf16[32,32,128]{2,1,0:T(8,128)(2,1)S(1)} async-done(((bf16[32,32,128]{2,1,0:T(8,128)(2,1)}), bf16[32,32,128]{2,1,0:T(8,128)(2,1)S(1)}, u32[]{:S(2)}, u32[]{:S(2)}) %all-to-all-start) | async-done | bytes 262176 | tf_op jit(solution)/shard_map/all_to_all | solution.py:121
  21.5 0.0 copy-done
  21.5 0.0 copy-done.2
  21.5 0.0 copy-done.1
  21.5 0.0 copy-done.4
  21.6 0.8 %shard_map.56.own_ref = f32[24,128]{1,0:T(8,128)S(1)} custom-call(bf16[32,32,128]{2,1,0:T(8,128)(2,1)S(1)} %all-to-all-done.src_ref, bf16[1024,1024]{1,0:T(8,128)(2,1)S(1)} %copy-done, f32[8,128]{1,0:T(8,128)S(1)} %rsqrt_bitcast_fusion.scale_ref, s32[16,1024]{1,0:T(8,128)S(1)} %bitcast.7, s32[8,128]{1,0:T(8,128)S(1)} %bitcast.11, s32[16,128]{1,0:T(8,128)S(1)} %bitcast.8), custom_call_target="tpu_custom_call" | custom-call | tf_op jit(solution)/shard_map/pallas_call | solution.py:111
  22.4 0.1 collective-permute-start
  22.5 1.2 %collective-permute-done.other_ref = f32[8,128]{1,0:T(8,128)S(1)} collective-permute-done((f32[8,128]{1,0:T(8,128)S(1)}, f32[8,128]{1,0:T(8,128)S(1)}, u32[]{:S(2)}, u32[]{:S(2)}) %collective-permute-start) | collective-permute-done | bytes 4128 | tf_op jit(solution)/shard_map/ppermute | solution.py:135
  23.6 11.8 %all_to_all.15.got_ref = f32[16,24,128]{2,1,0:T(8,128)S(1)} all-to-all(f32[16,24,128]{2,1,0:T(8,128)S(1)} %shard_map.57), channel_id=1, replica_groups={{20,22,16,18,12,14,8,10,4,6,0,2,28,30,24,26},{21,23,17,19,13,15,9,11,5,..., dimensions={0} | all-to-all | bytes 393216 | tf_op jit(solution)/shard_map/all_to_all | solution.py:121
  35.4 0.1 shard_map.58
  35.5 10.5 %all_to_all.16.got_ref = f32[8,32,128]{2,1,0:T(8,128)S(1)} all-to-all(f32[8,32,128]{2,1,0:T(8,128)S(1)} %shard_map.58), channel_id=1, replica_groups={{128,0,224,32,192,64,160,96},{129,1,225,33,193,65,161,97},{130,2,226,34..., dimensions={0} | all-to-all | bytes 262144 | tf_op jit(solution)/shard_map/all_to_all | solution.py:121
  46.1 0.6 %shard_map.59 = f32[16,128]{1,0:T(8,128)} custom-call(f32[8,32,128]{2,1,0:T(8,128)S(1)} %all_to_all.16.got_ref), custom_call_target="tpu_custom_call" | custom-call | tf_op jit(solution)/shard_map/pallas_call | solution.py:111
  (3 shorter events, 0.0 us)
Async XLA Ops:
  0.0 21.5 %copy-start = (bf16[1024,1024]{1,0:T(8,128)(2,1)S(1)}, bf16[1024,1024]{1,0:T(8,128)(2,1)}, u32[]{:S(2)}) copy-start(bf16[1024,1024]{1,0:T(8,128)(2,1)} %tgt_ref.1) | copy-start | bytes 6291460
  0.0 21.5 %copy-start.2 = (s32[128,16]{0,1:T(8,128)S(1)}, s32[128,16]{0,1:T(8,128)}, u32[]{:S(2)}) copy-start(s32[128,16]{0,1:T(8,128)} %param.7) | copy-start | bytes 24580
  0.0 21.5 %copy-start.1 = (s32[1024,16]{0,1:T(8,128)S(1)}, s32[1024,16]{0,1:T(8,128)}, u32[]{:S(2)}) copy-start(s32[1024,16]{0,1:T(8,128)} %param.8) | copy-start | bytes 196612
  0.0 0.8 %copy-start.3 = (bf16[128,32]{0,1:T(8,128)(2,1)S(1)}, bf16[128,32]{0,1:T(8,128)(2,1)}, u32[]{:S(2)}) copy-start(bf16[128,32]{0,1:T(8,128)(2,1)} %param.5) | copy-start | bytes 24580
  0.9 20.7 %copy-start.4 = (s32[1024]{0:T(1024)S(1)}, s32[1024]{0:T(1024)}, u32[]{:S(2)}) copy-start(s32[1024]{0:T(1024)} %param.9) | copy-start | bytes 12292
  1.6 19.9 %all-to-all-start = ((bf16[32,32,128]{2,1,0:T(8,128)(2,1)}), bf16[32,32,128]{2,1,0:T(8,128)(2,1)S(1)}, u32[]{:S(2)}, u32[]{:S(2)}) async-start(bf16[32,32,128]{2,1,0:T(8,128)(2,1)} %shard_map.55), calls=%async_computation | async-start | bytes 524288 | tf_op jit(solution)/shard_map/all_to_all | solution.py:121
  22.4 1.3 %collective-permute-start = (f32[8,128]{1,0:T(8,128)S(1)}, f32[8,128]{1,0:T(8,128)S(1)}, u32[]{:S(2)}, u32[]{:S(2)}) collective-permute-start(f32[8,128]{1,0:T(8,128)S(1)} %slice.4), channel_id=1, source_target_pairs={{0,1},{1,0},{2,3},{3,2},{4,5},{5,4},{6,7},{7,6},{8,9},{9,8},{10,11... | collective-permute-start | bytes 12296 | tf_op jit(solution)/shard_map/ppermute | solution.py:135

commit v10 on v7

--- a/solution.py
+++ b/solution.py
@@ -9,7 +9,7 @@
 TGT = ("z", "x")
 SRC = ("y", "core")
 GATHER = [((z + 4) % Z) * X + (x + 2) % X for x in (0, 3, 2, 1) for z in range(Z)]
-SUM = [((x + 2) % X) * Y + (y + 2) % Y for x in range(X) for y in range(Y)]
+SUM = [((x + 2) % X) * Y + (y + 2) % Y for x in (0, 3, 2, 1) for y in range(Y)]
 SPREAD = [(z + 4) % Z for z in (0, 4, 3, 5, 2, 6, 1, 7)]
 LANES = 128
 VMEM_BYTES = 24 * 1024 * 1024

time: 47 us -> 47 us (level)
  no operation moved by 1% of the time
where the time goes in v10:
time: 47 us; the launch traced here: 46.7 us
  blocking collectives  22.3 us (47%)
  starting transfers between devices  12.2 us (26%)
  waiting for transfers between devices  6.89 us (15%)
  other arithmetic  2.07 us (4%)
  local copies, waits for them, and re-layouts  1.59 us (3%)
  Pallas kernels  1.59 us (3%)
    all_to_all x2, blocking collectives, exchange(): return lax.all_to_all(blocks, axes, 0, 0, axis_index_groups=[order])  22.3 us
    all_to_all x1, starting transfers between devices, exchange(): return lax.all_to_all(blocks, axes, 0, 0, axis_index_groups=[order])  12.1 us
    all_to_all x1, waiting for transfers between devices, exchange(): return lax.all_to_all(blocks, axes, 0, 0, axis_index_groups=[order])  5.74 us
    reduce_sum x1, other arithmetic, body(): jnp.sum(tgt_float * tgt_float, axis=1) + 1e-06  2.07 us
    pallas_call x4, Pallas kernels, call(): pl.pallas_call(kernel, out_shape=jax.ShapeDtypeStruct(shape, jnp.float32)...  1.59 us
    broadcast_in_dim x1, local copies, waits for them, and re-layouts, body(): copies = jnp.broadcast_to(sources.T[None], (Z * X,) + sources.T.shape)  1.57 us
    ppermute x1, waiting for transfers between devices, body(): other = lax.ppermute(sent[:8], 'core', [(0, 1), (1, 0)])  1.15 us
  transfers between devices with their start and end apart: 2, of which 2 were waited for; matrix products, arithmetic and copies ran while one was open for 4% of the time, Pallas kernels for 0%

profile of v10, /device:TPU:2, one launch (start us, length us, event | category | flops | bytes accessed | tf_op | source)
XLA Modules:
  0.0 46.7 jit_solution(15809827931146700725)
XLA Ops:
  0.0 0.0 copy-start
  0.0 0.0 copy-start.2
  0.0 0.0 copy-start.1
  0.0 0.0 copy-start.3
  0.0 1.6 %broadcast_in_dim.2 = bf16[32,32,128]{2,1,0:T(8,128)(2,1)} broadcast(bf16[32,128]{1,0:T(8,128)(2,1)} %bitcast.11), dimensions={1,2} | broadcast | bytes 270336 | tf_op jit(solution)/shard_map/broadcast_in_dim | solution.py:121
  1.6 12.1 %all-to-all-start = ((bf16[32,32,128]{2,1,0:T(8,128)(2,1)}), bf16[32,32,128]{2,1,0:T(8,128)(2,1)S(1)}, u32[]{:S(2)}, u32[]{:S(2)}) async-start(bf16[32,32,128]{2,1,0:T(8,128)(2,1)} %broadcast_in_dim.2), calls=%async_computation | async-start | bytes 524288 | tf_op jit(solution)/shard_map/all_to_all | solution.py:115
  13.7 2.1 %multiply_reduce_fusion = f32[1024]{0:T(1024)S(1)} fusion(bf16[1024,1024]{1,0:T(8,128)(2,1)} %tgt_ref.1), kind=kLoop, calls=%fused_computation | loop fusion | flops 3144704 | bytes 2101248 | tf_op jit(solution)/shard_map/reduce_sum | solution.py:124
  15.8 5.7 %all-to-all-done.src_ref = bf16[32,32,128]{2,1,0:T(8,128)(2,1)S(1)} async-done(((bf16[32,32,128]{2,1,0:T(8,128)(2,1)}), bf16[32,32,128]{2,1,0:T(8,128)(2,1)S(1)}, u32[]{:S(2)}, u32[]{:S(2)}) %all-to-all-start) | async-done | bytes 262176 | tf_op jit(solution)/shard_map/all_to_all | solution.py:115
  21.5 0.0 copy-done
  21.5 0.0 copy-done.2
  21.5 0.0 copy-done.1
  21.5 0.0 copy-done.3
  21.6 0.8 %shard_map.55.own_ref = f32[24,128]{1,0:T(8,128)S(1)} custom-call(bf16[32,32,128]{2,1,0:T(8,128)(2,1)S(1)} %all-to-all-done.src_ref, bf16[1024,1024]{1,0:T(8,128)(2,1)S(1)} %copy-done, f32[8,128]{1,0:T(8,128)S(1)} %rsqrt_bitcast_fusion.scale_ref, s32[16,1024]{1,0:T(8,128)S(1)} %bitcast.7, s32[8,128]{1,0:T(8,128)S(1)} %bitcast.10, s32[16,128]{1,0:T(8,128)S(1)} %bitcast.8), custom_call_target="tpu_custom_call" | custom-call | tf_op jit(solution)/shard_map/pallas_call | solution.py:105
  22.4 0.1 collective-permute-start
  22.5 1.2 %collective-permute-done.other_ref = f32[8,128]{1,0:T(8,128)S(1)} collective-permute-done((f32[8,128]{1,0:T(8,128)S(1)}, f32[8,128]{1,0:T(8,128)S(1)}, u32[]{:S(2)}, u32[]{:S(2)}) %collective-permute-start) | collective-permute-done | bytes 4128 | tf_op jit(solution)/shard_map/ppermute | solution.py:129
  23.6 11.8 %all_to_all.15.got_ref = f32[16,24,128]{2,1,0:T(8,128)S(1)} all-to-all(f32[16,24,128]{2,1,0:T(8,128)S(1)} %shard_map.56), channel_id=1, replica_groups={{20,22,16,18,12,14,8,10,4,6,0,2,28,30,24,26},{21,23,17,19,13,15,9,11,5,..., dimensions={0} | all-to-all | bytes 393216 | tf_op jit(solution)/shard_map/all_to_all | solution.py:115
  35.4 0.1 shard_map.57
  35.5 10.5 %all_to_all.16.got_ref = f32[8,32,128]{2,1,0:T(8,128)S(1)} all-to-all(f32[8,32,128]{2,1,0:T(8,128)S(1)} %shard_map.57), channel_id=1, replica_groups={{128,0,224,32,192,64,160,96},{129,1,225,33,193,65,161,97},{130,2,226,34..., dimensions={0} | all-to-all | bytes 262144 | tf_op jit(solution)/shard_map/all_to_all | solution.py:115
  46.1 0.6 %shard_map.58 = f32[16,128]{1,0:T(8,128)} custom-call(f32[8,32,128]{2,1,0:T(8,128)S(1)} %all_to_all.16.got_ref), custom_call_target="tpu_custom_call" | custom-call | tf_op jit(solution)/shard_map/pallas_call | solution.py:105
  (3 shorter events, 0.0 us)
Async XLA Ops:
  0.0 21.5 %copy-start = (bf16[1024,1024]{1,0:T(8,128)(2,1)S(1)}, bf16[1024,1024]{1,0:T(8,128)(2,1)}, u32[]{:S(2)}) copy-start(bf16[1024,1024]{1,0:T(8,128)(2,1)} %tgt_ref.1) | copy-start | bytes 6291460
  0.0 21.5 %copy-start.2 = (s32[128,16]{0,1:T(8,128)S(1)}, s32[128,16]{0,1:T(8,128)}, u32[]{:S(2)}) copy-start(s32[128,16]{0,1:T(8,128)} %param.7) | copy-start | bytes 24580
  0.0 21.5 %copy-start.1 = (s32[1024,16]{0,1:T(8,128)S(1)}, s32[1024,16]{0,1:T(8,128)}, u32[]{:S(2)}) copy-start(s32[1024,16]{0,1:T(8,128)} %param.8) | copy-start | bytes 196612
  0.0 21.5 %copy-start.3 = (s32[1024]{0:T(1024)S(1)}, s32[1024]{0:T(1024)}, u32[]{:S(2)}) copy-start(s32[1024]{0:T(1024)} %param.9) | copy-start | bytes 12292
  1.6 19.9 %all-to-all-start = ((bf16[32,32,128]{2,1,0:T(8,128)(2,1)}), bf16[32,32,128]{2,1,0:T(8,128)(2,1)S(1)}, u32[]{:S(2)}, u32[]{:S(2)}) async-start(bf16[32,32,128]{2,1,0:T(8,128)(2,1)} %broadcast_in_dim.2), calls=%async_computation | async-start | bytes 524288 | tf_op jit(solution)/shard_map/all_to_all | solution.py:115
  22.4 1.3 %collective-permute-start = (f32[8,128]{1,0:T(8,128)S(1)}, f32[8,128]{1,0:T(8,128)S(1)}, u32[]{:S(2)}, u32[]{:S(2)}) collective-permute-start(f32[8,128]{1,0:T(8,128)S(1)} %slice.4), channel_id=1, source_target_pairs={{0,1},{1,0},{2,3},{3,2},{4,5},{5,4},{6,7},{7,6},{8,9},{9,8},{10,11... | collective-permute-start | bytes 12296 | tf_op jit(solution)/shard_map/ppermute | solution.py:129
